TPU v7x, 32 devices: a whole 2x2x4 slice. The times are simulated.
32 devices in a mesh: dp: 4 (over x, core), expert: 8 (over z, y).
Axes of the slice: x: 2, y: 2, z: 4, core: 2. Of those that a mesh axis runs over, the one named last changes fastest.
Arguments:
- embeds: bfloat16 [8192, 1152], P(('dp', 'expert')), may hold values from -6 to 6
- trunk_gain: float32 [1152], replicated, may hold values from 0.5 to 1.5
- trunk_weight: bfloat16 [1152, 1152], replicated, may hold values from -0.1875 to 0.1875
- w_gate: bfloat16 [32, 1152, 1024], P(('dp', 'expert')), may hold values from -0.1875 to 0.1875
- w_up: bfloat16 [32, 1152, 1024], P(('dp', 'expert')), may hold values from -0.1875 to 0.1875
- w_down: bfloat16 [32, 1024, 1152], P(('dp', 'expert')), may hold values from -0.1875 to 0.1875
- tags: int32 [8192], P(('dp', 'expert')), may hold values from 0 to 31, as said below
- plan: int32 [32], replicated, may hold values from 0 to 31, as said below
- helper: int32 [8192], P(('dp', 'expert')), may hold values from 0 to 31, as said below
- cotangent: bfloat16 [8192, 1152], P(('dp', 'expert')), may hold values from -0.59765625 to 0.59765625
Outputs:
- grad_gate: bfloat16 [32, 1152, 1024], P(('dp', 'expert'))
- grad_up: bfloat16 [32, 1152, 1024], P(('dp', 'expert'))
- grad_down: bfloat16 [32, 1024, 1152], P(('dp', 'expert'))
- grad_trunk: float32 [1152, 1152], P(('dp', 'expert'))
Inputs may be any that keep to these rules, and one draw needn't show every extreme that they name: Each token's helper equals its tag, except for tokens tagged with the expert plan[0], which may go to any device. Each device sends exactly 8 tokens to every device (numbered in the order dp then expert). Every device other than device plan[0] receives exactly 8 tokens tagged plan[0]; device plan[0] receives only tokens tagged plan[0]. `tags`: see helper. A permutation of the 32 experts; only plan[0] is served by helpers.
All inputs are finite; a program needn't handle non-finite values.
Results may differ from a plain program's by a relative error of at most 0.003.
The roundings to bfloat16 on the way count: a program that leaves them out, or rounds other values in their place, can miss the bound.
Values may be sent and summed in bfloat16 or wider, within the bound.
A program may use at most 128 MiB of HBM per device.

v0:
```python
import jax
import jax.numpy as jnp
from jax import lax
from jax.sharding import PartitionSpec as P


def expert_pass(rows, cotan, gate_w, up_w, down_w):
    gate_pre = jnp.dot(rows, gate_w, preferred_element_type=jnp.float32)
    up_pre = jnp.dot(rows, up_w, preferred_element_type=jnp.float32)
    sigma = jax.nn.sigmoid(gate_pre)
    silu_val = gate_pre * sigma
    active = (silu_val * up_pre).astype(jnp.bfloat16)
    d_active = jnp.dot(cotan, down_w.T, preferred_element_type=jnp.float32)
    d_gate = (d_active * up_pre * sigma * (1.0 + gate_pre * (1.0 - sigma))).astype(jnp.bfloat16)
    d_up = (d_active * silu_val).astype(jnp.bfloat16)
    sum_gate = jnp.dot(rows.T, d_gate, preferred_element_type=jnp.float32)
    sum_up = jnp.dot(rows.T, d_up, preferred_element_type=jnp.float32)
    sum_down = jnp.dot(active.T, cotan, preferred_element_type=jnp.float32)
    d_rows = jnp.dot(d_gate, gate_w.T, preferred_element_type=jnp.float32) + jnp.dot(
        d_up, up_w.T, preferred_element_type=jnp.float32
    )
    return (sum_gate, sum_up, sum_down, d_rows, active, d_gate, d_up)


def body(embeds, trunk_gain, trunk_weight, w_gate, w_up, w_down, tags, plan, helper, cotangent):
    devices = lax.axis_size(("dp", "expert"))
    device = lax.axis_index(("dp", "expert"))
    hot_expert = plan[0]
    tok_rows = embeds.shape[0]
    feature = embeds.shape[1]
    hidden_units = w_gate.shape[2]
    capacity = tok_rows // devices
    hot_slots = tok_rows // 32
    values = embeds.astype(jnp.float32)
    factor = lax.rsqrt(jnp.mean(values * values, axis=1, keepdims=True) + 1e-06)
    normed = (values * factor * trunk_gain).astype(jnp.bfloat16)
    hidden = (values + jnp.dot(normed, trunk_weight, preferred_element_type=jnp.float32)).astype(
        jnp.bfloat16
    )
    hits = (helper[:, None] == jnp.arange(devices, dtype=jnp.int32)[None, :]).astype(jnp.int32)
    earlier = jnp.cumsum(hits, axis=0) - hits
    slot_index = jnp.sum(earlier * hits, axis=1)
    position = helper * capacity + slot_index
    flagged = ((tags == hot_expert) & (helper != hot_expert)).astype(jnp.bfloat16)
    hidden_out = jnp.zeros_like(hidden).at[position].set(hidden)
    cotan_out = jnp.zeros_like(cotangent).at[position].set(cotangent)
    flag_out = jnp.zeros((tok_rows,), jnp.bfloat16).at[position].set(flagged)
    got_hidden, got_cotan, got_flag = (
        lax.all_to_all(
            hidden_out.reshape(devices, capacity, feature),
            ("dp", "expert"),
            split_axis=0,
            concat_axis=0,
            tiled=True,
        ),
        lax.all_to_all(
            cotan_out.reshape(devices, capacity, feature),
            ("dp", "expert"),
            split_axis=0,
            concat_axis=0,
            tiled=True,
        ),
        lax.all_to_all(
            flag_out.reshape(devices, capacity),
            ("dp", "expert"),
            split_axis=0,
            concat_axis=0,
            tiled=True,
        ),
    )
    recv_hidden = got_hidden.reshape(tok_rows, feature)
    recv_cotan = got_cotan.reshape(tok_rows, feature)
    recv_flag = got_flag.reshape(tok_rows)
    own_cotan = jnp.where(recv_flag[:, None] > 0, jnp.zeros_like(recv_cotan), recv_cotan)
    own_gate, own_up, own_down, own_drows, unused_act, unused_dg, unused_du = expert_pass(
        recv_hidden, own_cotan, w_gate[0], w_up[0], w_down[0]
    )
    flag_count = (recv_flag > 0).astype(jnp.int32)
    rank_hot = jnp.cumsum(flag_count) - flag_count
    picker = (rank_hot[None, :] == jnp.arange(hot_slots, dtype=jnp.int32)[:, None]) & (
        flag_count[None, :] > 0
    )
    picker_half = picker.astype(jnp.bfloat16)
    hot_rows = jnp.dot(picker_half, recv_hidden, preferred_element_type=jnp.float32).astype(
        jnp.bfloat16
    )
    hot_cotan = jnp.dot(picker_half, recv_cotan, preferred_element_type=jnp.float32).astype(
        jnp.bfloat16
    )
    is_owner = device == hot_expert
    aimed = jnp.arange(devices, dtype=jnp.int32) == hot_expert

    def toward_owner(block):
        return jnp.where(aimed[:, None, None], block[None], jnp.zeros_like(block)[None])

    zero_grads = (
        jnp.zeros((feature, hidden_units), jnp.float32),
        jnp.zeros((feature, hidden_units), jnp.float32),
        jnp.zeros((hidden_units, feature), jnp.float32),
    )
    came_rows, came_cotan = (
        lax.all_to_all(
            toward_owner(hot_rows), ("dp", "expert"), split_axis=0, concat_axis=0, tiled=True
        ),
        lax.all_to_all(
            toward_owner(hot_cotan), ("dp", "expert"), split_axis=0, concat_axis=0, tiled=True
        ),
    )
    pooled_rows = came_rows.reshape(devices * hot_slots, feature)
    pooled_cotan = came_cotan.reshape(devices * hot_slots, feature)

    def owner_pass():
        result = expert_pass(pooled_rows, pooled_cotan, w_gate[0], w_up[0], w_down[0])
        return (result[0], result[1], result[2], result[3])

    def helper_pass():
        return zero_grads + (jnp.zeros((devices * hot_slots, feature), jnp.float32),)

    total_gate, total_up, total_down, pooled_drows = lax.cond(is_owner, owner_pass, helper_pass)
    back = lax.all_to_all(
        pooled_drows.astype(jnp.bfloat16).reshape(devices, hot_slots, feature),
        ("dp", "expert"),
        split_axis=0,
        concat_axis=0,
        tiled=True,
    )
    hot_back = lax.dynamic_index_in_dim(back, hot_expert, 0, keepdims=False)
    returned = jnp.dot(picker_half.T, hot_back, preferred_element_type=jnp.float32)
    drows_send = (own_drows + returned).astype(jnp.bfloat16)
    grad_gate = jnp.where(is_owner, own_gate + total_gate, own_gate).astype(jnp.bfloat16)[None]
    grad_up = jnp.where(is_owner, own_up + total_up, own_up).astype(jnp.bfloat16)[None]
    grad_down = jnp.where(is_owner, own_down + total_down, own_down).astype(jnp.bfloat16)[None]
    came_back = lax.all_to_all(
        drows_send.reshape(devices, capacity, feature),
        ("dp", "expert"),
        split_axis=0,
        concat_axis=0,
        tiled=True,
    )
    dhidden = came_back.reshape(tok_rows, feature)[position]
    block = normed
    grad_trunk = lax.psum_scatter(
        jnp.dot(block.T, dhidden, preferred_element_type=jnp.float32),
        ("dp", "expert"),
        scatter_dimension=0,
        tiled=True,
    )
    return (grad_gate, grad_up, grad_down, grad_trunk)


def solution(mesh):
    placed = (
        P(("dp", "expert"), None),
        P(),
        P(),
        P(("dp", "expert"), None, None),
        P(("dp", "expert"), None, None),
        P(("dp", "expert"), None, None),
        P(("dp", "expert")),
        P(),
        P(("dp", "expert")),
        P(("dp", "expert"), None),
    )
    return jax.shard_map(
        body,
        mesh=mesh,
        in_specs=placed,
        out_specs=(
            P(("dp", "expert"), None, None),
            P(("dp", "expert"), None, None),
            P(("dp", "expert"), None, None),
            P(("dp", "expert"), None),
        ),
        check_vma=False,
    )
```

profile of v0, /device:TPU:28, one launch (start us, length us, event | category | flops | bytes accessed | tf_op | source)
XLA Modules:
  0.0 415.5 jit_solution(2205405450871083832)
XLA Ops:
  8.0 5.8 %all-to-all-start.1 = ((bf16[32,1,8]{2,1,0:T(2,128)(2,1)}), bf16[32,1,8]{2,1,0:T(2,128)(2,1)S(1)}, u32[]{:S(2)}, u32[]{:S(2)}) async-start(bf16[32,1,8]{2,1,0:T(2,128)(2,1)} %all_to_all.32), calls=%async_computation.1 | async-start | bytes 32768 | tf_op jit(solution)/shard_map/all_to_all | solution.py:63
  19.9 5.8 %all-to-all-start = ((bf16[32,8,1152]{2,1,0:T(8,128)(2,1)}), bf16[32,8,1152]{2,1,0:T(8,128)(2,1)S(1)}, u32[]{:S(2)}, u32[]{:S(2)}) async-start(bf16[32,8,1152]{2,1,0:T(8,128)(2,1)} %bitcast.10), calls=%async_computation | async-start | bytes 1179648 | tf_op jit(solution)/shard_map/all_to_all | solution.py:49
  25.8 3.0 scatter_custom_fusion.2
  28.8 11.9 %all-to-all-done = bf16[32,8,1152]{2,1,0:T(8,128)(2,1)S(1)} async-done(((bf16[32,8,1152]{2,1,0:T(8,128)(2,1)}), bf16[32,8,1152]{2,1,0:T(8,128)(2,1)S(1)}, u32[]{:S(2)}, u32[]{:S(2)}) %all-to-all-start) | async-done | bytes 589856 | tf_op jit(solution)/shard_map/all_to_all | solution.py:49
  40.7 6.1 %all-to-all-start.2 = ((bf16[32,8,1152]{2,1,0:T(8,128)(2,1)}), bf16[32,8,1152]{2,1,0:T(8,128)(2,1)}, u32[]{:S(2)}, u32[]{:S(2)}) async-start(bf16[32,8,1152]{2,1,0:T(8,128)(2,1)} %bitcast.13), calls=%async_computation.2 | async-start | bytes 1179648 | tf_op jit(solution)/shard_map/all_to_all | solution.py:56
  48.1 13.5 %all-to-all-done.2 = bf16[32,8,1152]{2,1,0:T(8,128)(2,1)} async-done(((bf16[32,8,1152]{2,1,0:T(8,128)(2,1)}), bf16[32,8,1152]{2,1,0:T(8,128)(2,1)}, u32[]{:S(2)}, u32[]{:S(2)}) %all-to-all-start.2) | async-done | bytes 589856 | tf_op jit(solution)/shard_map/all_to_all | solution.py:56
  63.9 20.1 %all_to_all.40 = bf16[32,8,1152]{2,1,0:T(8,128)(2,1)} all-to-all(bf16[32,8,1152]{2,1,0:T(8,128)(2,1)S(1)} %get-tuple-element.38), channel_id=1, replica_groups=mesh['dp'=4,'expert'=8] {'dp','expert'}, dimensions={0} | all-to-all | bytes 1179648 | tf_op jit(solution)/shard_map/all_to_all | solution.py:105
  84.0 6.2 %all-to-all-start.4 = ((bf16[32,8,1152]{2,1,0:T(8,128)(2,1)}), bf16[32,8,1152]{2,1,0:T(8,128)(2,1)}, u32[]{:S(2)}, u32[]{:S(2)}) async-start(bf16[32,8,1152]{2,1,0:T(8,128)(2,1)} %get-tuple-element.37), calls=%async_computation.4 | async-start | bytes 1179648 | tf_op jit(solution)/shard_map/all_to_all | solution.py:102
  92.3 12.8 %all-to-all-done.4 = bf16[32,8,1152]{2,1,0:T(8,128)(2,1)} async-done(((bf16[32,8,1152]{2,1,0:T(8,128)(2,1)}), bf16[32,8,1152]{2,1,0:T(8,128)(2,1)}, u32[]{:S(2)}, u32[]{:S(2)}) %all-to-all-start.4) | async-done | bytes 589856 | tf_op jit(solution)/shard_map/all_to_all | solution.py:102
  105.1 8.9 %conditional.1 = (f32[1024,1152]{1,0:T(8,128)}, bf16[256,1152]{1,0:T(8,128)(2,1)}, f32[1152,1024]{1,0:T(8,128)}, f32[1152,1024]{1,0:T(8,128)}) conditional(s32[]{:T(128)} %convert_element_type.85, () %tuple.16, (bf16[1,1024,1152]{2,1,0:T(8,128)(2,1)}, bf16[32,8,1152]{2,1,0:T(8,128)(2,1)}, bf16[1,1152,1024]{2,1,0:T(8,128)(2,1)}, ...), branch_computations={%region_9.10_spmd, %region_10.11_spmd} | conditional | flops 4837408768 | bytes 92471496 | solution.py:119
  105.1 2.7 broadcast.83.clone
  107.8 2.8 broadcast.83.clone2
  110.6 2.5 broadcast_in_dim.62
  114.0 29.3 %all-to-all-start.5 = ((bf16[32,8,1152]{2,1,0:T(8,128)(2,1)}), bf16[32,8,1152]{2,1,0:T(8,128)(2,1)}, u32[]{:S(2)}, u32[]{:S(2)}) async-start(bf16[32,8,1152]{2,1,0:T(8,128)(2,1)} %bitcast.106), calls=%async_computation.5 | async-start | bytes 1179648 | tf_op jit(solution)/shard_map/all_to_all | solution.py:120
  143.3 2.7 fusion.35
  146.0 3.4 multiply_convert_fusion.5
  152.1 6.1 %all-to-all-done.5 = bf16[32,8,1152]{2,1,0:T(8,128)(2,1)} async-done(((bf16[32,8,1152]{2,1,0:T(8,128)(2,1)}), bf16[32,8,1152]{2,1,0:T(8,128)(2,1)}, u32[]{:S(2)}, u32[]{:S(2)}) %all-to-all-start.5) | async-done | bytes 589856 | tf_op jit(solution)/shard_map/all_to_all | solution.py:120
  159.3 3.9 fusion.29
  163.3 5.5 %all-to-all-start.6 = ((bf16[32,8,1152]{2,1,0:T(8,128)(2,1)}), bf16[32,8,1152]{2,1,0:T(8,128)(2,1)S(1)}, u32[]{:S(2)}, u32[]{:S(2)}) async-start(bf16[32,8,1152]{2,1,0:T(8,128)(2,1)} %fusion.29), calls=%async_computation.6 | async-start | bytes 1179648 | tf_op jit(solution)/shard_map/all_to_all | solution.py:133
  168.8 5.4 %fusion.23 = bf16[1,1024,1152]{2,1,0:T(8,128)(2,1)} fusion(f32[1024,1152]{1,0:T(8,128)} %get-tuple-element.25, pred[]{:T(512)S(6)} %eq.55, bf16[32,8,1152]{2,1,0:T(8,128)(2,1)} %all-to-all-done.2, pred[256]{0:T(512)(128)(4,1)S(1)} %gt.40, f32[256,1024]{1,0:T(8,128)} %copy-done.14, f32[256,1024]{1,0:T(8,128)S(1)} %copy-done.13), kind=kOutput, calls=%fused_computation.35 | convolution fusion | flops 609386496 | bytes 9765121 | tf_op jit(solution)/shard_map/dot_general | solution.py:18
  174.1 9.4 %all-to-all-done.6 = bf16[32,8,1152]{2,1,0:T(8,128)(2,1)S(1)} async-done(((bf16[32,8,1152]{2,1,0:T(8,128)(2,1)}), bf16[32,8,1152]{2,1,0:T(8,128)(2,1)S(1)}, u32[]{:S(2)}, u32[]{:S(2)}) %all-to-all-start.6) | async-done | bytes 589856 | tf_op jit(solution)/shard_map/all_to_all | solution.py:133
  184.8 3.5 fusion.43
  188.3 155.4 %fusion = f32[48,1152]{1,0:T(8,128)S(1)} fusion(f32[1152,1152]{1,0:T(8,128)} %fusion.43), kind=kCustom, calls=%all-reduce-scatter | all-reduce-scatter fusion | flops 1769473 | bytes 5529600
  343.7 3.5 collective-permute-start
  349.1 4.4 %collective-permute-start.7 = (f32[36,1152]{1,0:T(8,128)S(1)}, f32[36,1152]{1,0:T(8,128)S(1)}, u32[]{:S(2)}, u32[]{:S(2)}) collective-permute-start(f32[36,1152]{1,0:T(8,128)S(1)} %slice.24), channel_id=1, source_target_pairs={{0,8},{1,9},{2,10},{3,11},{4,12},{5,13},{6,14},{7,15},{8,16},{9,17... | collective-permute-start | bytes 497672
  353.6 4.6 %fusion.24 = bf16[1,1152,1024]{2,1,0:T(8,128)(2,1)} fusion(f32[1152,1024]{1,0:T(8,128)} %get-tuple-element.30, bf16[256,1024]{1,0:T(8,128)(2,1)S(1)} %copy-done.9, pred[]{:T(512)S(6)} %eq.55, bf16[32,8,1152]{2,1,0:T(8,128)(2,1)S(1)} %all-to-all-done), kind=kOutput, calls=%fused_computation.36 | convolution fusion | flops 607518720 | bytes 8192001 | tf_op jit(solution)/shard_map/dot_general | solution.py:17
  358.2 2.9 collective-permute-start.2
  361.1 4.6 %collective-permute-start.3 = (f32[48,1152]{1,0:T(8,128)S(1)}, f32[48,1152]{1,0:T(8,128)S(1)}, u32[]{:S(2)}, u32[]{:S(2)}) collective-permute-start(f32[48,1152]{1,0:T(8,128)S(1)} %fusion), channel_id=1, source_target_pairs={{0,4},{1,5},{2,6},{3,7},{4,8},{5,9},{6,10},{7,11},{8,12},{9,13},{1... | collective-permute-start | bytes 663560
  371.6 4.7 %fusion.25 = bf16[1,1152,1024]{2,1,0:T(8,128)(2,1)} fusion(f32[1152,1024]{1,0:T(8,128)} %get-tuple-element.29, bf16[256,1024]{1,0:T(8,128)(2,1)S(1)} %copy-done.11, pred[]{:T(512)S(6)} %eq.55, bf16[32,8,1152]{2,1,0:T(8,128)(2,1)S(1)} %all-to-all-done), kind=kOutput, calls=%fused_computation.37 | convolution fusion | flops 607518720 | bytes 8192001 | tf_op jit(solution)/shard_map/dot_general | solution.py:16
  376.3 15.0 %collective-permute-done.3 = f32[48,1152]{1,0:T(8,128)S(1)} collective-permute-done((f32[48,1152]{1,0:T(8,128)S(1)}, f32[48,1152]{1,0:T(8,128)S(1)}, u32[]{:S(2)}, u32[]{:S(2)}) %collective-permute-start.3) | collective-permute-done | bytes 221216
  391.3 6.2 %collective-permute-done.4 = f32[48,1152]{1,0:T(8,128)S(1)} collective-permute-done((f32[48,1152]{1,0:T(8,128)S(1)}, f32[48,1152]{1,0:T(8,128)S(1)}, u32[]{:S(2)}, u32[]{:S(2)}) %collective-permute-start.4) | collective-permute-done | bytes 221216
  398.9 14.9 %concatenate = f32[420,1152]{1,0:T(8,128)} concatenate(f32[36,1152]{1,0:T(8,128)} %copy-done.21, f32[48,1152]{1,0:T(8,128)} %collective-permute-done.6, f32[48,1152]{1,0:T(8,128)} %copy-done.20, f32[48,1152]{1,0:T(8,128)} %copy-done.19, f32[48,1152]{1,0:T(8,128)} %copy-done.18, f32[48,1152]{1,0:T(8,128)} %copy-done.17, f32[48,1152]{1,0:T(8,128)} %copy-done.16, ...), dimensions={0} | concatenate | bytes 3870720
  (90 shorter events, 35.6 us)
Async XLA Ops:
  0.6 14.5 %copy-start = (bf16[1152,1152]{1,0:T(8,128)(2,1)S(1)}, bf16[1152,1152]{1,0:T(8,128)(2,1)}, u32[]{:S(2)}) copy-start(bf16[1152,1152]{1,0:T(8,128)(2,1)} %param.14) | copy-start | bytes 7962628
  8.0 11.9 %all-to-all-start.1 = ((bf16[32,1,8]{2,1,0:T(2,128)(2,1)}), bf16[32,1,8]{2,1,0:T(2,128)(2,1)S(1)}, u32[]{:S(2)}, u32[]{:S(2)}) async-start(bf16[32,1,8]{2,1,0:T(2,128)(2,1)} %all_to_all.32), calls=%async_computation.1 | async-start | bytes 32768 | tf_op jit(solution)/shard_map/all_to_all | solution.py:63
  17.4 29.4 %copy-start.23 = (s32[32]{0:T(128)S(1)}, s32[32]{0:T(128)}, u32[]{:S(2)}) copy-start(s32[32]{0:T(128)} %param.19) | copy-start | bytes 388
  19.9 20.7 %all-to-all-start = ((bf16[32,8,1152]{2,1,0:T(8,128)(2,1)}), bf16[32,8,1152]{2,1,0:T(8,128)(2,1)S(1)}, u32[]{:S(2)}, u32[]{:S(2)}) async-start(bf16[32,8,1152]{2,1,0:T(8,128)(2,1)} %bitcast.10), calls=%async_computation | async-start | bytes 1179648 | tf_op jit(solution)/shard_map/all_to_all | solution.py:49
  40.7 20.9 %all-to-all-start.2 = ((bf16[32,8,1152]{2,1,0:T(8,128)(2,1)}), bf16[32,8,1152]{2,1,0:T(8,128)(2,1)}, u32[]{:S(2)}, u32[]{:S(2)}) async-start(bf16[32,8,1152]{2,1,0:T(8,128)(2,1)} %bitcast.13), calls=%async_computation.2 | async-start | bytes 1179648 | tf_op jit(solution)/shard_map/all_to_all | solution.py:56
  47.9 42.6 %copy-start.2 = (bf16[1,1152,1024]{2,1,0:T(8,128)(2,1)S(1)}, bf16[1,1152,1024]{2,1,0:T(8,128)(2,1)}, u32[]{:S(2)}) copy-start(bf16[1,1152,1024]{2,1,0:T(8,128)(2,1)} %param.15) | copy-start | bytes 7077892
  84.0 21.1 %all-to-all-start.4 = ((bf16[32,8,1152]{2,1,0:T(8,128)(2,1)}), bf16[32,8,1152]{2,1,0:T(8,128)(2,1)}, u32[]{:S(2)}, u32[]{:S(2)}) async-start(bf16[32,8,1152]{2,1,0:T(8,128)(2,1)} %get-tuple-element.37), calls=%async_computation.4 | async-start | bytes 1179648 | tf_op jit(solution)/shard_map/all_to_all | solution.py:102
  114.0 44.2 %all-to-all-start.5 = ((bf16[32,8,1152]{2,1,0:T(8,128)(2,1)}), bf16[32,8,1152]{2,1,0:T(8,128)(2,1)}, u32[]{:S(2)}, u32[]{:S(2)}) async-start(bf16[32,8,1152]{2,1,0:T(8,128)(2,1)} %bitcast.106), calls=%async_computation.5 | async-start | bytes 1179648 | tf_op jit(solution)/shard_map/all_to_all | solution.py:120
  143.3 2.7 copy-start.12
  143.3 2.7 copy-start.24
  146.0 3.4 copy-start.14
  149.4 0.8 copy-start.10
  159.3 9.4 %copy-start.13 = (f32[256,1024]{1,0:T(8,128)S(1)}, f32[256,1024]{1,0:T(8,128)}, u32[]{:S(2)}) copy-start(f32[256,1024]{1,0:T(8,128)} %fusion.32) | copy-start | bytes 3145732
  163.3 20.2 %all-to-all-start.6 = ((bf16[32,8,1152]{2,1,0:T(8,128)(2,1)}), bf16[32,8,1152]{2,1,0:T(8,128)(2,1)S(1)}, u32[]{:S(2)}, u32[]{:S(2)}) async-start(bf16[32,8,1152]{2,1,0:T(8,128)(2,1)} %fusion.29), calls=%async_computation.6 | async-start | bytes 1179648 | tf_op jit(solution)/shard_map/all_to_all | solution.py:133
  183.5 1.3 copy-start.6
  183.5 1.3 copy-start.22
  188.3 165.2 %copy-start.9 = (bf16[256,1024]{1,0:T(8,128)(2,1)S(1)}, bf16[256,1024]{1,0:T(8,128)(2,1)}, u32[]{:S(2)}) copy-start(bf16[256,1024]{1,0:T(8,128)(2,1)} %get-tuple-element.35) | copy-start | bytes 1572868
  343.7 23.9 %collective-permute-start = (f32[48,1152]{1,0:T(8,128)S(1)}, f32[48,1152]{1,0:T(8,128)S(1)}, u32[]{:S(2)}, u32[]{:S(2)}) collective-permute-start(f32[48,1152]{1,0:T(8,128)S(1)} %fusion), channel_id=1, source_target_pairs={{0,1},{1,2},{2,3},{3,4},{4,5},{5,6},{6,7},{7,8},{8,9},{9,10},{10,1... | collective-permute-start | bytes 663560
  347.2 22.4 %collective-permute-start.1 = (f32[48,1152]{1,0:T(8,128)S(1)}, f32[48,1152]{1,0:T(8,128)S(1)}, u32[]{:S(2)}, u32[]{:S(2)}) collective-permute-start(f32[48,1152]{1,0:T(8,128)S(1)} %fusion), channel_id=1, source_target_pairs={{0,2},{1,3},{2,4},{3,5},{4,6},{5,7},{6,8},{7,9},{8,10},{9,11},{10,... | collective-permute-start | bytes 663560
  349.1 16.6 %collective-permute-start.7 = (f32[36,1152]{1,0:T(8,128)S(1)}, f32[36,1152]{1,0:T(8,128)S(1)}, u32[]{:S(2)}, u32[]{:S(2)}) collective-permute-start(f32[36,1152]{1,0:T(8,128)S(1)} %slice.24), channel_id=1, source_target_pairs={{0,8},{1,9},{2,10},{3,11},{4,12},{5,13},{6,14},{7,15},{8,16},{9,17... | collective-permute-start | bytes 497672
  353.5 18.0 %copy-start.11 = (bf16[256,1024]{1,0:T(8,128)(2,1)S(1)}, bf16[256,1024]{1,0:T(8,128)(2,1)}, u32[]{:S(2)}) copy-start(bf16[256,1024]{1,0:T(8,128)(2,1)} %copy-done.10) | copy-start | bytes 1572868
  358.2 18.1 %collective-permute-start.2 = (f32[48,1152]{1,0:T(8,128)S(1)}, f32[48,1152]{1,0:T(8,128)S(1)}, u32[]{:S(2)}, u32[]{:S(2)}) collective-permute-start(f32[48,1152]{1,0:T(8,128)S(1)} %fusion), channel_id=1, source_target_pairs={{0,3},{1,4},{2,5},{3,6},{4,7},{5,8},{6,9},{7,10},{8,11},{9,12},{10... | collective-permute-start | bytes 663560
  361.1 30.2 %collective-permute-start.3 = (f32[48,1152]{1,0:T(8,128)S(1)}, f32[48,1152]{1,0:T(8,128)S(1)}, u32[]{:S(2)}, u32[]{:S(2)}) collective-permute-start(f32[48,1152]{1,0:T(8,128)S(1)} %fusion), channel_id=1, source_target_pairs={{0,4},{1,5},{2,6},{3,7},{4,8},{5,9},{6,10},{7,11},{8,12},{9,13},{1... | collective-permute-start | bytes 663560
  365.7 5.9 %copy-start.21 = (f32[36,1152]{1,0:T(8,128)}, f32[36,1152]{1,0:T(8,128)S(1)}, u32[]{:S(2)}) copy-start(f32[36,1152]{1,0:T(8,128)S(1)} %collective-permute-done.7) | copy-start | bytes 497668
  365.7 31.8 %collective-permute-start.4 = (f32[48,1152]{1,0:T(8,128)S(1)}, f32[48,1152]{1,0:T(8,128)S(1)}, u32[]{:S(2)}, u32[]{:S(2)}) collective-permute-start(f32[48,1152]{1,0:T(8,128)S(1)} %fusion), channel_id=1, source_target_pairs={{0,5},{1,6},{2,7},{3,8},{4,9},{5,10},{6,11},{7,12},{8,13},{9,14},{... | collective-permute-start | bytes 663560
  367.6 2.0 copy-start.15
  367.7 29.9 %collective-permute-start.5 = (f32[48,1152]{1,0:T(8,128)S(1)}, f32[48,1152]{1,0:T(8,128)S(1)}, u32[]{:S(2)}, u32[]{:S(2)}) collective-permute-start(f32[48,1152]{1,0:T(8,128)S(1)} %fusion), channel_id=1, source_target_pairs={{0,6},{1,7},{2,8},{3,9},{4,10},{5,11},{6,12},{7,13},{8,14},{9,15},... | collective-permute-start | bytes 663560
  369.6 2.0 copy-start.16
  369.6 29.3 %collective-permute-start.6 = (f32[48,1152]{1,0:T(8,128)S(1)}, f32[48,1152]{1,0:T(8,128)}, u32[]{:S(2)}, u32[]{:S(2)}) collective-permute-start(f32[48,1152]{1,0:T(8,128)S(1)} %fusion), channel_id=1, source_target_pairs={{0,7},{1,8},{2,9},{3,10},{4,11},{5,12},{6,13},{7,14},{8,15},{9,16}... | collective-permute-start | bytes 663560
  371.6 43.9 %copy-start.1 = (bf16[1152,1152]{1,0:T(8,128)(2,1)S(1)}, bf16[1152,1152]{1,0:T(8,128)(2,1)}, u32[]{:S(2)}) copy-start(bf16[1152,1152]{1,0:T(8,128)(2,1)} %param.14) | copy-start | bytes 7962628
  376.3 21.2 %copy-start.17 = (f32[48,1152]{1,0:T(8,128)}, f32[48,1152]{1,0:T(8,128)S(1)}, u32[]{:S(2)}) copy-start(f32[48,1152]{1,0:T(8,128)S(1)} %collective-permute-done.2) | copy-start | bytes 663556
  391.3 6.3 %copy-start.18 = (f32[48,1152]{1,0:T(8,128)}, f32[48,1152]{1,0:T(8,128)S(1)}, u32[]{:S(2)}) copy-start(f32[48,1152]{1,0:T(8,128)S(1)} %collective-permute-done.3) | copy-start | bytes 663556
  (2 other events, 1.4 us)
where the time goes:
time: 417 us; the launch traced here: 415 us
  blocking collectives  175 us (42%)
  starting transfers between devices  81.8 us (20%)
  waiting for transfers between devices  74.9 us (18%)
  local copies, waits for them, and re-layouts  38.3 us (9%)
  matrix products  36.8 us (9%)
  other arithmetic  7.02 us (2%)
    unnamed x1, blocking collectives  155 us
    all_to_all x1, starting transfers between devices, body(): lax.all_to_all(pooled_drows.astype(jnp.bfloat16).reshape(devices, hot_slo...  29.3 us
    unnamed x8, starting transfers between devices  23 us
    unnamed x8, waiting for transfers between devices  21.2 us
    all_to_all x1, blocking collectives, body(): lax.all_to_all(toward_owner(hot_cotan), ('dp', 'expert'), split_axis=0, c...  20.1 us
    unnamed x43, local copies, waits for them, and re-layouts  18.8 us
    all_to_all x1, waiting for transfers between devices, body(): lax.all_to_all(cotan_out.reshape(devices, capacity, feature), ('dp', 'exp...  13.5 us
    all_to_all x1, waiting for transfers between devices, body(): lax.all_to_all(toward_owner(hot_rows), ('dp', 'expert'), split_axis=0, co...  12.8 us
  transfers between devices with their start and end apart: 14, of which 7 were waited for; matrix products, arithmetic and copies ran while one was open for 8% of the time, Pallas kernels for 0%

commit v1 on v0

v1 whole, which is shorter than its diff:
```python
import functools

import jax
import jax.numpy as jnp
from jax import lax
from jax.experimental import pallas as pl
from jax.experimental.pallas import tpu as pltpu
from jax.sharding import PartitionSpec as P

LANES = 128
TILE = 16
MESH = pl.DeviceIdType.MESH


def padded(value, multiple):
    return -(-value // multiple) * multiple


def flat_index(experts_axis):
    return lax.axis_index("dp") * experts_axis + lax.axis_index("expert")


def place(flat, experts_axis):
    return (flat // experts_axis, flat % experts_axis)


def flipped(me, bit):
    weight = 1 << bit
    return me + (1 - 2 * ((me // weight) % 2)) * weight


def greet_all(n, experts_axis):
    me = flat_index(experts_axis)
    barrier = pltpu.get_barrier_semaphore()

    def greet(step, carry):
        pl.semaphore_signal(
            barrier,
            inc=1,
            device_id=place(lax.rem(me + step, n), experts_axis),
            device_id_type=MESH,
        )
        return carry

    lax.fori_loop(1, n, greet, 0)
    pl.semaphore_wait(barrier, n - 1)


def greet_bits(bits, experts_axis):
    me = flat_index(experts_axis)
    barrier = pltpu.get_barrier_semaphore()
    for bit in range(bits):
        pl.semaphore_signal(
            barrier, inc=1, device_id=place(flipped(me, bit), experts_axis), device_id_type=MESH
        )
    pl.semaphore_wait(barrier, bits)


def exchange_kernel(n, experts_axis, send_ref, out_ref, send_sem, recv_sem, own_sem):
    me = flat_index(experts_axis)
    greet_all(n, experts_axis)
    own = pltpu.make_async_copy(send_ref.at[me], out_ref.at[me], own_sem)
    own.start()

    def copy_to(step):
        to = lax.rem(me + step, n)
        return pltpu.make_async_remote_copy(
            src_ref=send_ref.at[to],
            dst_ref=out_ref.at[me],
            send_sem=send_sem.at[to],
            recv_sem=recv_sem.at[me],
            device_id=place(to, experts_axis),
            device_id_type=MESH,
        )

    def copy_from(step):
        source = lax.rem(me + step, n)
        return pltpu.make_async_remote_copy(
            src_ref=send_ref.at[source],
            dst_ref=out_ref.at[source],
            send_sem=send_sem.at[source],
            recv_sem=recv_sem.at[source],
            device_id=place(source, experts_axis),
            device_id_type=MESH,
        )

    def start(step, carry):
        copy_to(step).start()
        return carry

    def finish(step, carry):
        copy = copy_from(step)
        copy.wait_send()
        copy.wait_recv()
        return carry

    lax.fori_loop(1, n, start, 0)
    own.wait()
    lax.fori_loop(1, n, finish, 0)


def exchange(send, n, experts_axis):
    return pl.pallas_call(
        functools.partial(exchange_kernel, n, experts_axis),
        out_shape=jax.ShapeDtypeStruct(send.shape, send.dtype),
        in_specs=[pl.BlockSpec(memory_space=pltpu.VMEM)],
        out_specs=pl.BlockSpec(memory_space=pltpu.VMEM),
        scratch_shapes=[
            pltpu.SemaphoreType.DMA((n,)),
            pltpu.SemaphoreType.DMA((n,)),
            pltpu.SemaphoreType.DMA,
        ],
        compiler_params=pltpu.CompilerParams(
            collective_id=0, has_side_effects=True, vmem_limit_bytes=40 * 1024 * 1024
        ),
    )(send)


def axis_orders(n, experts_axis):
    bits = n.bit_length() - 1
    core = experts_axis.bit_length() - 1
    others = [b for b in range(bits) if b != core]
    low = others[0]
    high = others[-1]
    middle = others[1:-1]
    return core, [
        [high, low] + middle,
        [low] + middle + [high],
        middle + [high, low],
    ]


def column_groups(width):
    tiles = width // LANES
    cuts = [(tiles * g) // 3 * LANES for g in range(4)]
    return [(cuts[g], cuts[g + 1] - cuts[g]) for g in range(3)]


def gather_kernel(n, experts_axis, width, mine_ref, out_ref, *scratch):
    bits = n.bit_length() - 1
    me = flat_index(experts_axis)
    core, orders = axis_orders(n, experts_axis)
    held, send_sem, recv_sem = scratch[:3], scratch[3], scratch[4]
    for group, (first, wide) in enumerate(column_groups(width)):
        held[group][0] = mine_ref[:, first : first + wide]
    greet_bits(bits, experts_axis)
    plans = [order[::-1] + [core] for order in orders]
    for stage in range(bits):
        count = 1 << stage
        copies = []
        for group in range(3):
            bit = plans[group][stage]
            copy = pltpu.make_async_remote_copy(
                src_ref=held[group].at[pl.ds(0, count)],
                dst_ref=held[group].at[pl.ds(count, count)],
                send_sem=send_sem.at[stage, group],
                recv_sem=recv_sem.at[stage, group],
                device_id=place(flipped(me, bit), experts_axis),
                device_id_type=MESH,
            )
            copy.start()
            copies.append(copy)
        for copy in copies:
            copy.wait()
    for group, (first, wide) in enumerate(column_groups(width)):
        for slot in range(n):
            offset = sum(
                1 << plans[group][stage] for stage in range(bits) if (slot >> stage) & 1
            )
            out_ref[offset, :, first : first + wide] = held[group][slot]


def gather(mine, n, experts_axis):
    rows, width = mine.shape
    bits = n.bit_length() - 1
    return pl.pallas_call(
        functools.partial(gather_kernel, n, experts_axis, width),
        out_shape=jax.ShapeDtypeStruct((n, rows, width), mine.dtype),
        in_specs=[pl.BlockSpec(memory_space=pltpu.VMEM)],
        out_specs=pl.BlockSpec(memory_space=pltpu.VMEM),
        scratch_shapes=[
            pltpu.VMEM((n, rows, wide), mine.dtype) for _, wide in column_groups(width)
        ]
        + [pltpu.SemaphoreType.DMA((bits, 3)), pltpu.SemaphoreType.DMA((bits, 3))],
        compiler_params=pltpu.CompilerParams(
            collective_id=1, has_side_effects=True, vmem_limit_bytes=48 * 1024 * 1024
        ),
    )(mine)


def stage_types(bits):
    return [jnp.bfloat16 if stage < 3 else jnp.float32 for stage in range(bits)]


def reduce_kernel(n, experts_axis, block, width, part_ref, out_ref, *scratch):
    bits = n.bit_length() - 1
    me = flat_index(experts_axis)
    core, orders = axis_orders(n, experts_axis)
    plans = [[core] + order for order in orders]
    groups = column_groups(width)
    types = stage_types(bits)
    sums = [[scratch[3 * (s * 3 + g)] for g in range(3)] for s in range(bits)]
    sent = [[scratch[3 * (s * 3 + g) + 1] for g in range(3)] for s in range(bits)]
    came = [[scratch[3 * (s * 3 + g) + 2] for g in range(3)] for s in range(bits)]
    send_sem, recv_sem = scratch[9 * bits], scratch[9 * bits + 1]
    greet_bits(bits, experts_axis)
    left = [sorted(range(bits), reverse=True) for _ in groups]
    for stage in range(bits):
        half = n >> (stage + 1)
        copies = []
        for group, (first, wide) in enumerate(groups):
            bit = plans[group][stage]
            low = 1 << (len(left[group]) - left[group].index(bit) - 1)
            mine = (me // (1 << bit)) % 2

            def read(item, side, low=low, stage=stage, group=group, first=first, wide=wide):
                at = (item // low) * (2 * low) + side * low + item % low
                if stage == 0:
                    return part_ref[at, :, first : first + wide]
                return sums[stage - 1][group][at]

            def pack(item, carry, read=read, mine=mine, stage=stage, group=group):
                sent[stage][group][item] = read(item, 1 - mine).astype(types[stage])
                return carry

            lax.fori_loop(0, half, pack, 0)
            copy = pltpu.make_async_remote_copy(
                src_ref=sent[stage][group],
                dst_ref=came[stage][group],
                send_sem=send_sem.at[stage, group],
                recv_sem=recv_sem.at[stage, group],
                device_id=place(flipped(me, bit), experts_axis),
                device_id_type=MESH,
            )
            copy.start()
            copies.append((copy, read, mine))
            left[group].remove(bit)
        for group in range(3):
            copy, read, mine = copies[group]
            copy.wait()

            def add(item, carry, read=read, mine=mine, stage=stage, group=group):
                sums[stage][group][item] = read(item, mine) + came[stage][group][item].astype(
                    jnp.float32
                )
                return carry

            lax.fori_loop(0, half, add, 0)
    for group, (first, wide) in enumerate(groups):
        out_ref[:, first : first + wide] = sums[bits - 1][group][0]


def reduce_scatter(part, n, experts_axis):
    block, width = part.shape[1:]
    bits = n.bit_length() - 1
    types = stage_types(bits)
    scratch = []
    for stage in range(bits):
        half = n >> (stage + 1)
        for _, wide in column_groups(width):
            scratch.append(pltpu.VMEM((half, block, wide), jnp.float32))
            scratch.append(pltpu.VMEM((half, block, wide), types[stage]))
            scratch.append(pltpu.VMEM((half, block, wide), types[stage]))
    return pl.pallas_call(
        functools.partial(reduce_kernel, n, experts_axis, block, width),
        out_shape=jax.ShapeDtypeStruct((block, width), jnp.float32),
        in_specs=[pl.BlockSpec(memory_space=pltpu.VMEM)],
        out_specs=pl.BlockSpec(memory_space=pltpu.VMEM),
        scratch_shapes=scratch
        + [pltpu.SemaphoreType.DMA((bits, 3)), pltpu.SemaphoreType.DMA((bits, 3))],
        compiler_params=pltpu.CompilerParams(
            collective_id=2, has_side_effects=True, vmem_limit_bytes=52 * 1024 * 1024
        ),
    )(part)


def lines_of(blocks, count, rows, first):
    lines = blocks.shape[0]
    wanted = jnp.arange(lines // rows * count, dtype=jnp.int32)
    wanted = wanted // count * rows + first + wanted % count
    chosen = wanted[:, None] == jnp.arange(lines, dtype=jnp.int32)[None, :]
    return jnp.dot(
        chosen.astype(jnp.bfloat16), blocks, preferred_element_type=jnp.float32
    ).astype(jnp.bfloat16)


def trunk(rows, gain, weight):
    values = rows.astype(jnp.float32)
    factor = lax.rsqrt(jnp.mean(values * values, axis=1, keepdims=True) + 1e-06)
    normed = (values * factor * gain).astype(jnp.bfloat16)
    hidden = values + jnp.dot(normed, weight, preferred_element_type=jnp.float32)
    return normed, hidden.astype(jnp.bfloat16)


def dot_t(a, b):
    return lax.dot_general(a, b, (((1,), (1,)), ((), ())), preferred_element_type=jnp.float32)


def t_dot(a, b):
    return lax.dot_general(a, b, (((0,), (0,)), ((), ())), preferred_element_type=jnp.float32)


def through_expert(hidden, cotan, gate_w, up_w, down_w):
    gate_pre = jnp.dot(hidden, gate_w, preferred_element_type=jnp.float32)
    up_pre = jnp.dot(hidden, up_w, preferred_element_type=jnp.float32)
    sigma = jax.nn.sigmoid(gate_pre)
    silu_val = gate_pre * sigma
    active = (silu_val * up_pre).astype(jnp.bfloat16)
    d_active = dot_t(cotan, down_w)
    d_gate = (d_active * up_pre * sigma * (1.0 + gate_pre * (1.0 - sigma))).astype(jnp.bfloat16)
    d_up = (d_active * silu_val).astype(jnp.bfloat16)
    d_rows = (dot_t(d_gate, gate_w) + dot_t(d_up, up_w)).astype(jnp.bfloat16)
    return active, d_gate, d_up, d_rows


def body(embeds, trunk_gain, trunk_weight, w_gate, w_up, w_down, tags, plan, helper, cotangent):
    n = lax.axis_size(("dp", "expert"))
    experts_axis = lax.axis_size("expert")
    device = flat_index(experts_axis)
    hot_expert = plan[0]
    tokens, feature = embeds.shape
    capacity = tokens // n
    hot_slots = tokens // 32
    rows = padded(2 * capacity, TILE)
    gate_w, up_w, down_w = w_gate[0], w_up[0], w_down[0]

    token = jnp.arange(tokens, dtype=jnp.int32)
    before = (helper[:, None] == helper[None, :]) & (token[:, None] > token[None, :])
    slot = jnp.sum(before.astype(jnp.int32), axis=1)
    target = helper * rows + slot
    line = jnp.arange(n * rows, dtype=jnp.int32)
    pick = jnp.concatenate(
        [line[:, None] == target[None, :], line[:, None] == target[None, :] + capacity], axis=1
    ).astype(jnp.bfloat16)
    flagged = ((tags == hot_expert) & (helper != hot_expert)).astype(jnp.bfloat16)
    flag_lanes = jnp.broadcast_to(flagged[:, None], (tokens, LANES))
    content = jnp.concatenate(
        [
            jnp.concatenate([embeds, flag_lanes], axis=1),
            jnp.concatenate([cotangent, jnp.zeros_like(flag_lanes)], axis=1),
        ],
        axis=0,
    )
    send = jnp.dot(pick, content, preferred_element_type=jnp.float32).astype(jnp.bfloat16)
    got = exchange(send.reshape(n, rows, feature + LANES), n, experts_axis)
    got = got.reshape(n * rows, feature + LANES)
    got_wide = lines_of(got, capacity, rows, 0)
    got_embeds = got_wide[:, :feature]
    got_cotan = lines_of(got[:, :feature], capacity, rows, capacity)
    flags = got_wide[:, feature] > 0

    rank = jnp.sum((flags[None, :] & (token[:, None] > token[None, :])).astype(jnp.int32), axis=1)
    picker = (rank[None, :] == jnp.arange(hot_slots, dtype=jnp.int32)[:, None]) & flags[None, :]
    picker = picker.astype(jnp.bfloat16)
    hot = jnp.concatenate(
        [
            jnp.dot(picker, got_embeds, preferred_element_type=jnp.float32),
            jnp.dot(picker, got_cotan, preferred_element_type=jnp.float32),
        ],
        axis=0,
    ).astype(jnp.bfloat16)
    pooled = gather(hot, n, experts_axis)
    pooled = pooled.reshape(n * 2 * hot_slots, feature)
    hot_embeds = lines_of(pooled, hot_slots, 2 * hot_slots, 0)
    hot_cotan = lines_of(pooled, hot_slots, 2 * hot_slots, hot_slots)
    is_owner = device == hot_expert
    hot_cotan = jnp.where(is_owner, hot_cotan, jnp.zeros_like(hot_cotan))
    own_cotan = jnp.where(flags[:, None], jnp.zeros_like(got_cotan), got_cotan)

    all_embeds = jnp.concatenate([got_embeds, hot_embeds], axis=0)
    all_cotan = jnp.concatenate([own_cotan, hot_cotan], axis=0)
    normed, hidden = trunk(all_embeds, trunk_gain, trunk_weight)
    active, d_gate, d_up, d_rows = through_expert(hidden, all_cotan, gate_w, up_w, down_w)

    share = feature // n
    block = padded(share, TILE)
    spread = jnp.pad(
        normed.reshape(normed.shape[0], n, share), ((0, 0), (0, 0), (0, block - share))
    ).reshape(normed.shape[0], n * block)
    part = t_dot(spread, d_rows).reshape(n, block, feature)
    grad_trunk = reduce_scatter(part, n, experts_axis)[:share]

    grad_gate = t_dot(hidden, d_gate).astype(jnp.bfloat16)[None]
    grad_up = t_dot(hidden, d_up).astype(jnp.bfloat16)[None]
    grad_down = t_dot(active, all_cotan).astype(jnp.bfloat16)[None]
    return (grad_gate, grad_up, grad_down, grad_trunk)


def solution(mesh):
    spread_rows = P(("dp", "expert"), None)
    spread_first = P(("dp", "expert"), None, None)
    return jax.shard_map(
        body,
        mesh=mesh,
        in_specs=(
            spread_rows,
            P(),
            P(),
            spread_first,
            spread_first,
            spread_first,
            P(("dp", "expert")),
            P(),
            P(("dp", "expert")),
            spread_rows,
        ),
        out_specs=(spread_first, spread_first, spread_first, spread_rows),
        check_vma=False,
    )
```

time: 417 us -> 147 us (0.35)
  the two profiles are of different devices: /device:TPU:28 before, /device:TPU:0 now
where the time goes in v1:
time: 147 us; the launch traced here: 146 us
  Pallas kernels  93.2 us (63%)
  matrix products  37.1 us (25%)
  local copies, waits for them, and re-layouts  8.03 us (5%)
  other arithmetic  6.34 us (4%)
  between operations  1.66 us (1%)
    pallas_call x1, Pallas kernels, reduce_scatter(): pl.pallas_call(functools.partial(reduce_kernel, n, experts_axis, block, w...  36.9 us
    pallas_call x1, Pallas kernels, exchange(): pl.pallas_call(functools.partial(exchange_kernel, n, experts_axis), out_s...  35.5 us
    pallas_call x1, Pallas kernels, gather(): pl.pallas_call(functools.partial(gather_kernel, n, experts_axis, width),...  20.8 us
    dot_general x4, matrix products, t_dot(): lax.dot_general(a, b, (((0,), (0,)), ((), ())), preferred_element_type=jn...  18.3 us
    dot_general x2, matrix products, dot_t(): lax.dot_general(a, b, (((1,), (1,)), ((), ())), preferred_element_type=jn...  5.09 us
    dot_general x4, matrix products, lines_of(): jnp.dot(chosen.astype(jnp.bfloat16), blocks, preferred_element_type=jnp.f...  3.84 us
    concatenate x2, local copies, waits for them, and re-layouts, body(): all_embeds = jnp.concatenate([got_embeds, hot_embeds], axis=0)  3.34 us

profile of v1, /device:TPU:0, one launch (start us, length us, event | category | flops | bytes accessed | tf_op | source)
XLA Modules:
  0.0 146.4 jit_solution(16952473406068334012)
XLA Ops:
  1.4 1.3 and_convert_fusion
  2.8 0.9 convert_reduce_fusion.1
  3.7 0.7 broadcast_add_fusion
  4.4 0.8 mul.94
  5.5 2.1 %convolution_convert_fusion.3 = bf16[512,1280]{1,0:T(8,128)(2,1)S(1)} fusion(bf16[256,1152]{1,0:T(8,128)(2,1)} %param.19, bf16[256,128]{1,0:T(8,128)(2,1)S(1)} %broadcast_in_dim.13, bf16[256,1152]{1,0:T(8,128)(2,1)} %param.10, pred[512,256]{1,0:T(32,128)(4,1)S(1)} %get-tuple-element.10, pred[512,256]{1,0:T(32,128)(4,1)S(1)} %get-tuple-element.11), kind=kOutput, calls=%fused_computation.12 | convolution fusion | flops 677249024 | bytes 2818048 | tf_op jit(solution)/shard_map/dot_general | solution.py:344
  7.6 35.5 %shard_map.129 = bf16[32,16,1280]{2,1,0:T(8,128)(2,1)S(1)} custom-call(bf16[32,16,1280]{2,1,0:T(8,128)(2,1)S(1)} %bitcast.60), custom_call_target="tpu_custom_call" | custom-call | tf_op jit(solution)/shard_map/pallas_call | solution.py:103
  43.1 0.5 convolution_convert_fusion.7
  43.8 1.4 broadcast_select_fusion
  45.2 0.2 convolution_convert_fusion.8
  45.4 0.2 convolution_convert_fusion.9
  45.7 1.1 copy.17
  46.8 2.0 %concatenate.36 = bf16[256,32,36]{0,2,1:T(8,128)(2,1)} reshape(bf16[256,1152]{0,1:T(8,128)(2,1)} %copy.17) | data formatting | bytes 1179648 | tf_op jit(solution)/shard_map/concatenate | solution.py:370
  48.8 20.8 %shard_map.130 = bf16[32,16,1152]{2,1,0:T(8,128)(2,1)S(1)} custom-call(bf16[16,1152]{1,0:T(8,128)(2,1)S(1)} %pad_maximum_fusion.5.mine_ref), custom_call_target="tpu_custom_call" | custom-call | tf_op jit(solution)/shard_map/pallas_call | solution.py:176
  69.6 1.4 fusion.7
  71.0 0.5 convolution_convert_fusion.5
  71.6 0.5 copy-done.2
  72.1 0.3 fusion.8
  72.4 2.9 %fusion.3 = bf16[512,1152]{1,0:T(8,128)(2,1)} fusion(bf16[1152,1152]{1,0:T(8,128)(2,1)S(1)} %copy-done, f32[1152]{0:T(1024)S(1)} %copy-done.3, f32[512]{0:T(512)S(1)} %add_rsqrt_fusion, bf16[256,1152]{1,0:T(8,128)(2,1)S(1)} %convolution_convert_fusion.5, bf16[256,1152]{1,0:T(8,128)(2,1)S(1)} %copy-done.2), kind=kOutput, calls=%fused_computation.10 | convolution fusion | flops 1366622208 | bytes 5020160 | tf_op jit(solution)/shard_map/dot_general | solution.py:291
  75.3 1.1 copy.18
  76.4 1.4 concatenate.37
  77.8 2.7 %multiply_convert_fusion = bf16[512,32,36]{0,2,1:T(8,128)(2,1)} fusion(bf16[256,32,36]{0,2,1:T(8,128)(2,1)S(1)} %concatenate.37, bf16[256,32,36]{0,2,1:T(8,128)(2,1)} %concatenate.36, f32[32,36]{1,0:T(8,128)S(1)} %mul.94, f32[512]{0:T(512)S(1)} %add_rsqrt_fusion), kind=kLoop, calls=%fused_computation.15 | loop fusion | flops 4128768 | bytes 2365952 | tf_op jit(solution)/shard_map/convert_element_type | solution.py:290
  80.4 2.9 %fusion.13 = f32[512,1024]{1,0:T(8,128)S(1)} fusion(bf16[512,1152]{1,0:T(8,128)(2,1)} %fusion.3, bf16[1,1152,1024]{2,1,0:T(8,128)(2,1)S(1)} %copy-done.5), kind=kOutput, calls=%fused_computation.27 | convolution fusion | flops 1207959552 | bytes 5636096 | tf_op jit(solution)/shard_map/dot_general | solution.py:304
  83.4 1.6 %fusion.16 = f32[512,1024]{1,0:T(8,128)S(1)} fusion(bf16[512,1152]{1,0:T(8,128)(2,1)S(1)} %copy-done.9, bf16[1,1152,1024]{2,1,0:T(8,128)(2,1)S(1)} %copy-done.6), kind=kOutput, calls=%fused_computation.30 | convolution fusion | flops 1207959552 | bytes 5636096 | tf_op jit(solution)/shard_map/dot_general | solution.py:305
  85.2 0.2 copy-done.8
  85.4 2.1 %multiply_convert_fusion.2 = (bf16[512,1024]{1,0:T(8,128)(2,1)S(1)}, bf16[512,1024]{1,0:T(8,128)(2,1)S(1)}) fusion(f32[512,1024]{1,0:T(8,128)S(1)} %fusion.13, f32[512,1024]{1,0:T(8,128)S(1)} %fusion.16, bf16[1,1024,1152]{2,1,0:T(8,128)(2,1)S(1)} %copy-done.4, bf16[256,1152]{1,0:T(8,128)(2,1)S(1)} %copy-done.7, bf16[256,1152]{1,0:T(8,128)(2,1)S(1)} %copy-done.8), kind=kOutput, calls=%fused_computation.37 | convolution fusion | flops 1217134592 | bytes 9830400 | tf_op jit(solution)/shard_map/dot_general | solution.py:296
  87.4 3.1 %fusion.2 = bf16[1,1024,1152]{2,1,0:T(8,128)(2,1)} fusion(f32[512,1024]{1,0:T(8,128)S(1)} %fusion.16, bf16[256,1152]{1,0:T(8,128)(2,1)S(1)} %copy-done.7, bf16[256,1152]{1,0:T(8,128)(2,1)S(1)} %copy-done.8, f32[512,1024]{1,0:T(8,128)S(1)} %fusion.13), kind=kOutput, calls=%fused_computation.9 | convolution fusion | flops 1214644224 | bytes 7733248 | tf_op jit(solution)/shard_map/dot_general | solution.py:300
  90.5 2.8 %fusion.1 = bf16[1,1152,1024]{2,1,0:T(8,128)(2,1)} fusion(bf16[512,1152]{1,0:T(8,128)(2,1)S(1)} %copy-done.9, bf16[512,1024]{1,0:T(8,128)(2,1)S(1)} %get-tuple-element.6), kind=kOutput, calls=%fused_computation.8 | convolution fusion | flops 1209139200 | bytes 4587520 | tf_op jit(solution)/shard_map/dot_general | solution.py:300
  93.3 2.8 %fusion = bf16[1,1152,1024]{2,1,0:T(8,128)(2,1)} fusion(bf16[512,1152]{1,0:T(8,128)(2,1)S(1)} %copy-done.9, bf16[512,1024]{1,0:T(8,128)(2,1)S(1)} %get-tuple-element.7), kind=kOutput, calls=%fused_computation.7 | convolution fusion | flops 1209139200 | bytes 4587520 | tf_op jit(solution)/shard_map/dot_general | solution.py:300
  96.2 3.0 %fusion.11 = f32[512,1152]{1,0:T(8,128)} fusion(bf16[512,1024]{1,0:T(8,128)(2,1)S(1)} %get-tuple-element.7, bf16[1,1152,1024]{2,1,0:T(8,128)(2,1)S(1)} %copy-done.5), kind=kOutput, calls=%fused_computation.25 | convolution fusion | flops 1207959552 | bytes 5767168 | tf_op jit(solution)/shard_map/dot_general | solution.py:296
  99.2 9.6 %fusion.22.part_ref = f32[32,48,1152]{2,1,0:T(8,128)} fusion(bf16[512,32,36]{0,2,1:T(8,128)(2,1)} %multiply_convert_fusion, f32[512,1152]{1,0:T(8,128)} %fusion.11, bf16[512,1024]{1,0:T(8,128)(2,1)} %copy-done.10, bf16[1,1152,1024]{2,1,0:T(8,128)(2,1)} %param.14), kind=kOutput, calls=%fused_computation.41 | convolution fusion | flops 3021078528 | bytes 14024704 | tf_op jit(solution)/shard_map/dot_general | solution.py:300
  108.8 36.9 %shard_map.131 = f32[48,1152]{1,0:T(8,128)S(1)} custom-call(f32[32,48,1152]{2,1,0:T(8,128)} %fusion.22.part_ref), custom_call_target="tpu_custom_call" | custom-call | tf_op jit(solution)/shard_map/pallas_call | solution.py:264
  145.7 0.7 slice.19
  (29 shorter events, 0.8 us)
Async XLA Ops:
  0.6 71.8 %copy-start = (bf16[1152,1152]{1,0:T(8,128)(2,1)S(1)}, bf16[1152,1152]{1,0:T(8,128)(2,1)}, u32[]{:S(2)}) copy-start(bf16[1152,1152]{1,0:T(8,128)(2,1)} %param.12) | copy-start | bytes 7962628
  45.7 23.9 %copy-start.1 = (bf16[256,1152]{1,0:T(8,128)(2,1)}, bf16[256,1152]{1,0:T(8,128)(2,1)S(1)}, u32[]{:S(2)}) copy-start(bf16[256,1152]{1,0:T(8,128)(2,1)S(1)} %slice.20) | copy-start | bytes 1769476
  69.6 2.8 %copy-start.3 = (f32[1152]{0:T(1024)S(1)}, f32[1152]{0:T(1024)}, u32[]{:S(2)}) copy-start(f32[1152]{0:T(1024)} %param.11) | copy-start | bytes 13828
  71.0 1.1 copy-start.2
  77.8 2.7 %copy-start.5 = (bf16[1,1152,1024]{2,1,0:T(8,128)(2,1)S(1)}, bf16[1,1152,1024]{2,1,0:T(8,128)(2,1)}, u32[]{:S(2)}) copy-start(bf16[1,1152,1024]{2,1,0:T(8,128)(2,1)} %param.13) | copy-start | bytes 7077892
  80.4 2.9 %copy-start.6 = (bf16[1,1152,1024]{2,1,0:T(8,128)(2,1)S(1)}, bf16[1,1152,1024]{2,1,0:T(8,128)(2,1)}, u32[]{:S(2)}) copy-start(bf16[1,1152,1024]{2,1,0:T(8,128)(2,1)} %param.14) | copy-start | bytes 7077892
  80.4 3.0 %copy-start.9 = (bf16[512,1152]{1,0:T(8,128)(2,1)S(1)}, bf16[512,1152]{1,0:T(8,128)(2,1)}, u32[]{:S(2)}) copy-start(bf16[512,1152]{1,0:T(8,128)(2,1)} %fusion.3) | copy-start | bytes 3538948
  83.4 1.7 %copy-start.4 = (bf16[1,1024,1152]{2,1,0:T(8,128)(2,1)S(1)}, bf16[1,1024,1152]{2,1,0:T(8,128)(2,1)}, u32[]{:S(2)}) copy-start(bf16[1,1024,1152]{2,1,0:T(8,128)(2,1)} %param.15) | copy-start | bytes 7077892
  83.4 1.8 %copy-start.7 = (bf16[256,1152]{1,0:T(8,128)(2,1)S(1)}, bf16[256,1152]{1,0:T(8,128)(2,1)}, u32[]{:S(2)}) copy-start(bf16[256,1152]{1,0:T(8,128)(2,1)} %fusion.7) | copy-start | bytes 1769476
  83.4 1.9 %copy-start.8 = (bf16[256,1152]{1,0:T(8,128)(2,1)S(1)}, bf16[256,1152]{1,0:T(8,128)(2,1)}, u32[]{:S(2)}) copy-start(bf16[256,1152]{1,0:T(8,128)(2,1)} %get-tuple-element.8) | copy-start | bytes 1769476
  87.4 3.1 %copy-start.10 = (bf16[512,1024]{1,0:T(8,128)(2,1)}, bf16[512,1024]{1,0:T(8,128)(2,1)S(1)}, u32[]{:S(2)}) copy-start(bf16[512,1024]{1,0:T(8,128)(2,1)S(1)} %get-tuple-element.6) | copy-start | bytes 3145732

commit v2 on v1

--- a/solution.py
+++ b/solution.py
@@ -192,66 +192,88 @@
     return [jnp.bfloat16 if stage < 3 else jnp.float32 for stage in range(bits)]
 
 
-def reduce_kernel(n, experts_axis, block, width, part_ref, out_ref, *scratch):
+def reduce_kernel(n, experts_axis, block, width, left_ref, right_ref, out_ref, *scratch):
     bits = n.bit_length() - 1
     me = flat_index(experts_axis)
     core, orders = axis_orders(n, experts_axis)
     plans = [[core] + order for order in orders]
     groups = column_groups(width)
     types = stage_types(bits)
-    sums = [[scratch[3 * (s * 3 + g)] for g in range(3)] for s in range(bits)]
+    kept = [[scratch[3 * (s * 3 + g)] for g in range(3)] for s in range(bits)]
     sent = [[scratch[3 * (s * 3 + g) + 1] for g in range(3)] for s in range(bits)]
     came = [[scratch[3 * (s * 3 + g) + 2] for g in range(3)] for s in range(bits)]
     send_sem, recv_sem = scratch[9 * bits], scratch[9 * bits + 1]
     greet_bits(bits, experts_axis)
-    left = [sorted(range(bits), reverse=True) for _ in groups]
-    for stage in range(bits):
+
+    def transfer(stage, group):
+        return pltpu.make_async_remote_copy(
+            src_ref=sent[stage][group],
+            dst_ref=came[stage][group],
+            send_sem=send_sem.at[stage, group],
+            recv_sem=recv_sem.at[stage, group],
+            device_id=place(flipped(me, plans[group][stage]), experts_axis),
+            device_id_type=MESH,
+        )
+
+    def side_of(bit):
+        return (me // (1 << bit)) % 2
+
+    chunk = experts_axis * block
+    spans = n // (2 * experts_axis)
+
+    def first_half(group, side, into, kind):
+        first, wide = groups[group]
+        for span in range(spans):
+            at = pl.multiple_of((2 * span + side) * chunk, chunk)
+            product = jnp.dot(
+                left_ref[pl.ds(at, chunk), :],
+                right_ref[:, first : first + wide],
+                preferred_element_type=jnp.float32,
+            )
+            for item in range(experts_axis):
+                into[span * experts_axis + item] = product[
+                    item * block : (item + 1) * block
+                ].astype(kind)
+
+    for group in range(3):
+        first_half(group, 1 - side_of(core), sent[0][group], types[0])
+        transfer(0, group).start()
+    for group in range(3):
+        first_half(group, side_of(core), kept[0][group], jnp.float32)
+
+    left = [[b for b in range(bits - 1, -1, -1) if b != core] for _ in groups]
+    for stage in range(1, bits):
         half = n >> (stage + 1)
-        copies = []
-        for group, (first, wide) in enumerate(groups):
+        for group in range(3):
             bit = plans[group][stage]
             low = 1 << (len(left[group]) - left[group].index(bit) - 1)
-            mine = (me // (1 << bit)) % 2
-
-            def read(item, side, low=low, stage=stage, group=group, first=first, wide=wide):
-                at = (item // low) * (2 * low) + side * low + item % low
-                if stage == 0:
-                    return part_ref[at, :, first : first + wide]
-                return sums[stage - 1][group][at]
-
-            def pack(item, carry, read=read, mine=mine, stage=stage, group=group):
-                sent[stage][group][item] = read(item, 1 - mine).astype(types[stage])
-                return carry
-
-            lax.fori_loop(0, half, pack, 0)
-            copy = pltpu.make_async_remote_copy(
-                src_ref=sent[stage][group],
-                dst_ref=came[stage][group],
-                send_sem=send_sem.at[stage, group],
-                recv_sem=recv_sem.at[stage, group],
-                device_id=place(flipped(me, bit), experts_axis),
-                device_id_type=MESH,
-            )
-            copy.start()
-            copies.append((copy, read, mine))
             left[group].remove(bit)
-        for group in range(3):
-            copy, read, mine = copies[group]
-            copy.wait()
-
-            def add(item, carry, read=read, mine=mine, stage=stage, group=group):
-                sums[stage][group][item] = read(item, mine) + came[stage][group][item].astype(
-                    jnp.float32
-                )
-                return carry
-
-            lax.fori_loop(0, half, add, 0)
+            mine = side_of(bit)
+
+            def move(side, into, kind, low=low, stage=stage, group=group, half=half):
+                def one(item, carry):
+                    at = (item // low) * (2 * low) + side * low + item % low
+                    into[item] = (
+                        kept[stage - 1][group][at]
+                        + came[stage - 1][group][at].astype(jnp.float32)
+                    ).astype(kind)
+                    return carry
+
+                lax.fori_loop(0, half, one, 0)
+
+            transfer(stage - 1, group).wait()
+            move(1 - mine, sent[stage][group], types[stage])
+            transfer(stage, group).start()
+            move(mine, kept[stage][group], jnp.float32)
     for group, (first, wide) in enumerate(groups):
-        out_ref[:, first : first + wide] = sums[bits - 1][group][0]
-
-
-def reduce_scatter(part, n, experts_axis):
-    block, width = part.shape[1:]
+        transfer(bits - 1, group).wait()
+        out_ref[:, first : first + wide] = kept[bits - 1][group][0] + came[bits - 1][group][
+            0
+        ].astype(jnp.float32)
+
+
+def reduce_scatter(left, right, block, n, experts_axis):
+    width = right.shape[1]
     bits = n.bit_length() - 1
     types = stage_types(bits)
     scratch = []
@@ -264,14 +286,14 @@
     return pl.pallas_call(
         functools.partial(reduce_kernel, n, experts_axis, block, width),
         out_shape=jax.ShapeDtypeStruct((block, width), jnp.float32),
-        in_specs=[pl.BlockSpec(memory_space=pltpu.VMEM)],
+        in_specs=[pl.BlockSpec(memory_space=pltpu.VMEM)] * 2,
         out_specs=pl.BlockSpec(memory_space=pltpu.VMEM),
         scratch_shapes=scratch
         + [pltpu.SemaphoreType.DMA((bits, 3)), pltpu.SemaphoreType.DMA((bits, 3))],
         compiler_params=pltpu.CompilerParams(
             collective_id=2, has_side_effects=True, vmem_limit_bytes=52 * 1024 * 1024
         ),
-    )(part)
+    )(left, right)
 
 
 def lines_of(blocks, count, rows, first):
@@ -373,12 +395,14 @@
     active, d_gate, d_up, d_rows = through_expert(hidden, all_cotan, gate_w, up_w, down_w)
 
     share = feature // n
-    block = padded(share, TILE)
-    spread = jnp.pad(
-        normed.reshape(normed.shape[0], n, share), ((0, 0), (0, 0), (0, block - share))
-    ).reshape(normed.shape[0], n * block)
-    part = t_dot(spread, d_rows).reshape(n, block, feature)
-    grad_trunk = reduce_scatter(part, n, experts_axis)[:share]
+    block = padded(share, TILE // 2)
+    column = jnp.arange(n * block, dtype=jnp.int32)
+    source = jnp.where(column % block < share, column // block * share + column % block, -1)
+    spread = (source[:, None] == jnp.arange(feature, dtype=jnp.int32)[None, :]).astype(
+        jnp.bfloat16
+    )
+    normed_lines = dot_t(spread, normed).astype(jnp.bfloat16)
+    grad_trunk = reduce_scatter(normed_lines, d_rows, block, n, experts_axis)[:share]
 
     grad_gate = t_dot(hidden, d_gate).astype(jnp.bfloat16)[None]
     grad_up = t_dot(hidden, d_up).astype(jnp.bfloat16)[None]

time: 147 us -> 122 us (0.83)
  matrix products: 37.1 us -> 26.9 us
  local copies, waits for them, and re-layouts: 8.03 us -> 1.1 us
  Pallas kernels: 93.2 us -> 88.3 us
  other arithmetic: 6.34 us -> 3.69 us
    dot_general x4 -> x3, matrix products: 18.3 us -> 8.91 us  [t_dot(): lax.dot_general(a, b, (((0,), (0,)), ((), ())), preferred_element_type=jn...]
    pallas_call x1, Pallas kernels: 36.9 us -> 32 us  [reduce_scatter(): pl.pallas_call(functools.partial(reduce_kernel, n, experts_axis, block, w...]
    concatenate x2 -> x0, local copies, waits for them, and re-layouts: 3.34 us -> none  [body(): all_embeds = jnp.concatenate([got_embeds, hot_embeds], axis=0)]
    dot_general x2 -> x4, matrix products: 5.09 us -> 8.3 us  [dot_t(): lax.dot_general(a, b, (((1,), (1,)), ((), ())), preferred_element_type=jn...]
    convert_element_type x1 -> x0, other arithmetic: 2.66 us -> none  [trunk(): normed = (values * factor * gain).astype(jnp.bfloat16)]
    dot_general x4, matrix products: 3.84 us -> 2.21 us  [lines_of(): jnp.dot(chosen.astype(jnp.bfloat16), blocks, preferred_element_type=jnp.f...]
where the time goes in v2:
time: 122 us
  Pallas kernels  88.3 us (72%)
  matrix products  26.9 us (22%)
  other arithmetic  3.69 us (3%)
  between operations  1.62 us (1%)
    pallas_call x1, Pallas kernels, exchange(): pl.pallas_call(functools.partial(exchange_kernel, n, experts_axis), out_s...  35.5 us
    pallas_call x1, Pallas kernels, reduce_scatter(): pl.pallas_call(functools.partial(reduce_kernel, n, experts_axis, block, w...  32 us
    pallas_call x1, Pallas kernels, gather(): pl.pallas_call(functools.partial(gather_kernel, n, experts_axis, width),...  20.8 us
    dot_general x3, matrix products, t_dot(): lax.dot_general(a, b, (((0,), (0,)), ((), ())), preferred_element_type=jn...  8.91 us
    dot_general x4, matrix products, dot_t(): lax.dot_general(a, b, (((1,), (1,)), ((), ())), preferred_element_type=jn...  8.3 us

profile of v2, /device:TPU:0, one launch (start us, length us, event | category | flops | bytes accessed | tf_op | source)
XLA Modules:
  0.0 121.6 jit_solution(13947391710105746773)
XLA Ops:
  1.4 1.3 %and_convert_fusion = bf16[256]{0:T(256)(128)(2,1)S(1)} fusion(s32[256]{0:T(256)} %param.18, s32[256]{0:T(256)} %param.16, s32[]{:T(128)} %bitcast.47), kind=kLoop, calls=%fused_computation.101 | loop fusion | flops 1024 | bytes 2564 | tf_op jit(solution)/shard_map/convert_element_type | solution.py:357
  2.8 0.9 convert_reduce_fusion.1
  3.7 0.7 broadcast_add_fusion
  4.4 0.1 broadcast_in_dim.14
  4.5 0.2 iota_compare_fusion.8
  4.7 2.1 %convolution_convert_fusion.3 = bf16[512,1280]{1,0:T(8,128)(2,1)S(1)} fusion(bf16[256,1152]{1,0:T(8,128)(2,1)} %param.19, bf16[256,128]{1,0:T(8,128)(2,1)S(1)} %broadcast_in_dim.14, bf16[256,1152]{1,0:T(8,128)(2,1)} %param.10, pred[512,256]{1,0:T(32,128)(4,1)S(1)} %get-tuple-element.10, pred[512,256]{1,0:T(32,128)(4,1)S(1)} %get-tuple-element.11), kind=kOutput, calls=%fused_computation.14 | convolution fusion | flops 677249024 | bytes 2818048 | tf_op jit(solution)/shard_map/dot_general | solution.py:366
  6.8 35.5 %shard_map.129 = bf16[32,16,1280]{2,1,0:T(8,128)(2,1)S(1)} custom-call(bf16[32,16,1280]{2,1,0:T(8,128)(2,1)S(1)} %bitcast.44), custom_call_target="tpu_custom_call" | custom-call | tf_op jit(solution)/shard_map/pallas_call | solution.py:103
  42.3 0.5 convolution_convert_fusion.7
  42.9 0.1 compare_reduce_fusion
  43.0 0.6 broadcast_select_fusion
  43.5 0.1 convert_reduce_fusion
  43.7 0.2 convolution_convert_fusion.8
  43.8 0.2 convolution_convert_fusion.9
  44.1 0.1 slice.20
  44.1 20.8 %shard_map.130 = bf16[32,16,1152]{2,1,0:T(8,128)(2,1)S(1)} custom-call(bf16[16,1152]{1,0:T(8,128)(2,1)S(1)} %pad_maximum_fusion.6.mine_ref), custom_call_target="tpu_custom_call" | custom-call | tf_op jit(solution)/shard_map/pallas_call | solution.py:176
  64.9 0.6 fusion.9
  65.5 0.6 convolution_convert_fusion.5
  66.1 0.3 fusion.10
  66.4 1.9 %fusion.4 = bf16[512,1152]{1,0:T(8,128)(2,1)S(1)} fusion(bf16[1152,1152]{1,0:T(8,128)(2,1)S(1)} %copy-done, f32[1152]{0:T(1024)S(1)} %copy-done.4, f32[512]{0:T(512)S(1)} %add_rsqrt_fusion, bf16[256,1152]{1,0:T(8,128)(2,1)S(1)} %convolution_convert_fusion.5, bf16[256,1152]{1,0:T(8,128)(2,1)S(1)} %slice.20), kind=kOutput, calls=%fused_computation.12 | convolution fusion | flops 1366622208 | bytes 5020160 | tf_op jit(solution)/shard_map/dot_general | solution.py:313
  68.3 3.1 %fusion.6.left_ref = bf16[1280,512]{1,0:T(8,128)(2,1)} fusion(s32[1280]{0:T(1024)S(1)} %fusion.56, f32[1152]{0:T(1024)S(1)} %copy-done.4, f32[512]{0:T(512)S(1)} %add_rsqrt_fusion, bf16[256,1152]{1,0:T(8,128)(2,1)S(1)} %convolution_convert_fusion.5, bf16[256,1152]{1,0:T(8,128)(2,1)S(1)} %slice.20), kind=kOutput, calls=%fused_computation.15 | convolution fusion | flops 1516208128 | bytes 2502144 | tf_op jit(solution)/shard_map/dot_general | solution.py:318
  71.4 1.6 %fusion.15 = f32[512,1024]{1,0:T(8,128)S(1)} fusion(bf16[512,1152]{1,0:T(8,128)(2,1)S(1)} %fusion.4, bf16[1,1152,1024]{2,1,0:T(8,128)(2,1)S(1)} %copy-done.2), kind=kOutput, calls=%fused_computation.29 | convolution fusion | flops 1207959552 | bytes 5636096 | tf_op jit(solution)/shard_map/dot_general | solution.py:326
  73.0 0.1 copy-done.3
  73.1 1.5 %fusion.18 = f32[512,1024]{1,0:T(8,128)S(1)} fusion(bf16[512,1152]{1,0:T(8,128)(2,1)S(1)} %fusion.4, bf16[1,1152,1024]{2,1,0:T(8,128)(2,1)S(1)} %copy-done.3), kind=kOutput, calls=%fused_computation.32 | convolution fusion | flops 1207959552 | bytes 5636096 | tf_op jit(solution)/shard_map/dot_general | solution.py:327
  74.6 0.1 copy-done.1
  74.8 2.1 %multiply_convert_fusion.1 = (bf16[512,1024]{1,0:T(8,128)(2,1)S(1)}, bf16[512,1024]{1,0:T(8,128)(2,1)S(1)}) fusion(f32[512,1024]{1,0:T(8,128)S(1)} %fusion.15, f32[512,1024]{1,0:T(8,128)S(1)} %fusion.18, bf16[1,1024,1152]{2,1,0:T(8,128)(2,1)S(1)} %copy-done.1, bf16[256,1152]{1,0:T(8,128)(2,1)S(1)} %fusion.9, bf16[256,1152]{1,0:T(8,128)(2,1)S(1)} %get-tuple-element.8), kind=kOutput, calls=%fused_computation.39 | convolution fusion | flops 1217134592 | bytes 9830400 | tf_op jit(solution)/shard_map/dot_general | solution.py:318
  76.8 3.1 %fusion.3 = bf16[1,1024,1152]{2,1,0:T(8,128)(2,1)} fusion(f32[512,1024]{1,0:T(8,128)S(1)} %fusion.18, bf16[256,1152]{1,0:T(8,128)(2,1)S(1)} %fusion.9, bf16[256,1152]{1,0:T(8,128)(2,1)S(1)} %get-tuple-element.8, f32[512,1024]{1,0:T(8,128)S(1)} %fusion.15), kind=kOutput, calls=%fused_computation.11 | convolution fusion | flops 1214644224 | bytes 7733248 | tf_op jit(solution)/shard_map/dot_general | solution.py:322
  79.9 3.0 %fusion.2 = bf16[1,1152,1024]{2,1,0:T(8,128)(2,1)} fusion(bf16[512,1152]{1,0:T(8,128)(2,1)S(1)} %fusion.4, bf16[512,1024]{1,0:T(8,128)(2,1)S(1)} %get-tuple-element.6), kind=kOutput, calls=%fused_computation.10 | convolution fusion | flops 1209139200 | bytes 4587520 | tf_op jit(solution)/shard_map/dot_general | solution.py:322
  82.9 2.8 %fusion.1 = bf16[1,1152,1024]{2,1,0:T(8,128)(2,1)} fusion(bf16[512,1152]{1,0:T(8,128)(2,1)S(1)} %fusion.4, bf16[512,1024]{1,0:T(8,128)(2,1)S(1)} %get-tuple-element.7), kind=kOutput, calls=%fused_computation.9 | convolution fusion | flops 1209139200 | bytes 4587520 | tf_op jit(solution)/shard_map/dot_general | solution.py:322
  85.7 1.6 %fusion.13 = f32[512,1152]{1,0:T(8,128)S(1)} fusion(bf16[512,1024]{1,0:T(8,128)(2,1)S(1)} %get-tuple-element.7, bf16[1,1152,1024]{2,1,0:T(8,128)(2,1)S(1)} %copy-done.2), kind=kOutput, calls=%fused_computation.27 | convolution fusion | flops 1207959552 | bytes 5767168 | tf_op jit(solution)/shard_map/dot_general | solution.py:318
  87.3 1.6 %fusion.5.right_ref = bf16[512,1152]{1,0:T(8,128)(2,1)S(1)} fusion(f32[512,1152]{1,0:T(8,128)S(1)} %fusion.13, bf16[512,1024]{1,0:T(8,128)(2,1)S(1)} %get-tuple-element.6, bf16[1,1152,1024]{2,1,0:T(8,128)(2,1)S(1)} %copy-done.3), kind=kOutput, calls=%fused_computation.13 | convolution fusion | flops 1209139200 | bytes 6946816 | tf_op jit(solution)/shard_map/dot_general | solution.py:318
  88.9 32.0 %shard_map.131 = f32[40,1152]{1,0:T(8,128)S(1)} custom-call(bf16[1280,512]{1,0:T(8,128)(2,1)} %fusion.6.left_ref, bf16[512,1152]{1,0:T(8,128)(2,1)S(1)} %fusion.5.right_ref), custom_call_target="tpu_custom_call" | custom-call | tf_op jit(solution)/shard_map/pallas_call | solution.py:286
  120.9 0.7 copy.19
  (13 shorter events, 0.1 us)
Async XLA Ops:
  0.6 65.7 %copy-start = (bf16[1152,1152]{1,0:T(8,128)(2,1)S(1)}, bf16[1152,1152]{1,0:T(8,128)(2,1)}, u32[]{:S(2)}) copy-start(bf16[1152,1152]{1,0:T(8,128)(2,1)} %param.12) | copy-start | bytes 7962628
  64.9 1.5 %copy-start.4 = (f32[1152]{0:T(1024)S(1)}, f32[1152]{0:T(1024)}, u32[]{:S(2)}) copy-start(f32[1152]{0:T(1024)} %param.11) | copy-start | bytes 13828
  68.3 3.1 %copy-start.2 = (bf16[1,1152,1024]{2,1,0:T(8,128)(2,1)S(1)}, bf16[1,1152,1024]{2,1,0:T(8,128)(2,1)}, u32[]{:S(2)}) copy-start(bf16[1,1152,1024]{2,1,0:T(8,128)(2,1)} %param.13) | copy-start | bytes 7077892
  71.4 1.7 %copy-start.3 = (bf16[1,1152,1024]{2,1,0:T(8,128)(2,1)S(1)}, bf16[1,1152,1024]{2,1,0:T(8,128)(2,1)}, u32[]{:S(2)}) copy-start(bf16[1,1152,1024]{2,1,0:T(8,128)(2,1)} %param.14) | copy-start | bytes 7077892
  73.1 1.7 %copy-start.1 = (bf16[1,1024,1152]{2,1,0:T(8,128)(2,1)S(1)}, bf16[1,1024,1152]{2,1,0:T(8,128)(2,1)}, u32[]{:S(2)}) copy-start(bf16[1,1024,1152]{2,1,0:T(8,128)(2,1)} %param.15) | copy-start | bytes 7077892

commit v3 on v2

--- a/solution.py
+++ b/solution.py
@@ -136,8 +136,82 @@
     return [(cuts[g], cuts[g + 1] - cuts[g]) for g in range(3)]
 
 
-def gather_kernel(n, experts_axis, width, mine_ref, out_ref, *scratch):
+def tile_of(width):
+    tile = 3 * LANES
+    while width % tile:
+        tile -= LANES
+    return tile
+
+
+def contract_last(a, b):
+    return lax.dot_general(a, b, (((1,), (1,)), ((), ())), preferred_element_type=jnp.float32)
+
+
+def own_steps(ins, outs):
+    rows_ref, cotan_ref, gain_ref, trunk_ref, gate_ref, up_ref, down_ref = ins
+    normed_ref, hidden_ref, act_ref, dgate_ref, dup_ref, drows_ref = outs
+    feature = rows_ref.shape[1]
+    units = gate_ref.shape[1]
+    wide = tile_of(feature)
+    deep = tile_of(units)
+
+    def trunk_step():
+        values = rows_ref[...].astype(jnp.float32)
+        factor = lax.rsqrt(jnp.mean(values * values, axis=1, keepdims=True) + 1e-06)
+        normed_ref[...] = (values * factor * gain_ref[...]).astype(jnp.bfloat16)
+
+        def one(tile, carry):
+            at = pl.ds(pl.multiple_of(tile * wide, wide), wide)
+            hidden_ref[:, at] = (
+                rows_ref[:, at].astype(jnp.float32)
+                + jnp.dot(normed_ref[...], trunk_ref[:, at], preferred_element_type=jnp.float32)
+            ).astype(jnp.bfloat16)
+            return carry
+
+        lax.fori_loop(0, feature // wide, one, 0)
+
+    def expert_step(first, last):
+        def one(tile, carry):
+            at = pl.ds(pl.multiple_of(tile * deep, deep), deep)
+            gate_pre = jnp.dot(
+                hidden_ref[...], gate_ref[:, at], preferred_element_type=jnp.float32
+            )
+            up_pre = jnp.dot(hidden_ref[...], up_ref[:, at], preferred_element_type=jnp.float32)
+            sigma = jax.nn.sigmoid(gate_pre)
+            silu_val = gate_pre * sigma
+            d_active = contract_last(cotan_ref[...], down_ref[at, :])
+            act_ref[:, at] = (silu_val * up_pre).astype(jnp.bfloat16)
+            dgate_ref[:, at] = (
+                d_active * up_pre * sigma * (1.0 + gate_pre * (1.0 - sigma))
+            ).astype(jnp.bfloat16)
+            dup_ref[:, at] = (d_active * silu_val).astype(jnp.bfloat16)
+            return carry
+
+        lax.fori_loop(first, last, one, 0)
+
+    def rows_step():
+        def one(tile, carry):
+            at = pl.ds(pl.multiple_of(tile * wide, wide), wide)
+            drows_ref[:, at] = (
+                contract_last(dgate_ref[...], gate_ref[at, :])
+                + contract_last(dup_ref[...], up_ref[at, :])
+            ).astype(jnp.bfloat16)
+            return carry
+
+        lax.fori_loop(0, feature // wide, one, 0)
+
+    tiles = units // deep
+    return [
+        trunk_step,
+        lambda: expert_step(0, tiles // 2),
+        lambda: expert_step(tiles // 2, tiles),
+        rows_step,
+    ]
+
+
+def gather_kernel(n, experts_axis, width, mine_ref, *refs):
     bits = n.bit_length() - 1
+    ins, out_ref, outs, scratch = refs[:7], refs[7], refs[8:14], refs[14:]
     me = flat_index(experts_axis)
     core, orders = axis_orders(n, experts_axis)
     held, send_sem, recv_sem = scratch[:3], scratch[3], scratch[4]
@@ -145,6 +219,7 @@
         held[group][0] = mine_ref[:, first : first + wide]
     greet_bits(bits, experts_axis)
     plans = [order[::-1] + [core] for order in orders]
+    steps = own_steps(ins, outs)
     for stage in range(bits):
         count = 1 << stage
         copies = []
@@ -160,6 +235,8 @@
             )
             copy.start()
             copies.append(copy)
+        if stage < len(steps):
+            steps[stage]()
         for copy in copies:
             copy.wait()
     for group, (first, wide) in enumerate(column_groups(width)):
@@ -170,14 +247,17 @@
             out_ref[offset, :, first : first + wide] = held[group][slot]
 
 
-def gather(mine, n, experts_axis):
+def gather(mine, own, n, experts_axis):
     rows, width = mine.shape
     bits = n.bit_length() - 1
+    tokens, units = own[0].shape[0], own[4].shape[1]
+    shapes = [(n, rows, width), (tokens, width), (tokens, width)]
+    shapes += [(tokens, units)] * 3 + [(tokens, width)]
     return pl.pallas_call(
         functools.partial(gather_kernel, n, experts_axis, width),
-        out_shape=jax.ShapeDtypeStruct((n, rows, width), mine.dtype),
-        in_specs=[pl.BlockSpec(memory_space=pltpu.VMEM)],
-        out_specs=pl.BlockSpec(memory_space=pltpu.VMEM),
+        out_shape=[jax.ShapeDtypeStruct(shape, mine.dtype) for shape in shapes],
+        in_specs=[pl.BlockSpec(memory_space=pltpu.VMEM)] * 8,
+        out_specs=[pl.BlockSpec(memory_space=pltpu.VMEM)] * 7,
         scratch_shapes=[
             pltpu.VMEM((n, rows, wide), mine.dtype) for _, wide in column_groups(width)
         ]
@@ -185,7 +265,7 @@
         compiler_params=pltpu.CompilerParams(
             collective_id=1, has_side_effects=True, vmem_limit_bytes=48 * 1024 * 1024
         ),
-    )(mine)
+    )(mine, *own)
 
 
 def stage_types(bits):
@@ -381,18 +461,20 @@
         ],
         axis=0,
     ).astype(jnp.bfloat16)
-    pooled = gather(hot, n, experts_axis)
+    own_cotan = jnp.where(flags[:, None], jnp.zeros_like(got_cotan), got_cotan)
+    own = (got_embeds, own_cotan, trunk_gain[None], trunk_weight, gate_w, up_w, down_w)
+    pooled, *own_parts = gather(hot, own, n, experts_axis)
     pooled = pooled.reshape(n * 2 * hot_slots, feature)
     hot_embeds = lines_of(pooled, hot_slots, 2 * hot_slots, 0)
     hot_cotan = lines_of(pooled, hot_slots, 2 * hot_slots, hot_slots)
     is_owner = device == hot_expert
     hot_cotan = jnp.where(is_owner, hot_cotan, jnp.zeros_like(hot_cotan))
-    own_cotan = jnp.where(flags[:, None], jnp.zeros_like(got_cotan), got_cotan)
-
-    all_embeds = jnp.concatenate([got_embeds, hot_embeds], axis=0)
+    hot_parts = trunk(hot_embeds, trunk_gain, trunk_weight)
+    hot_parts = hot_parts + through_expert(hot_parts[1], hot_cotan, gate_w, up_w, down_w)
+    normed, hidden, active, d_gate, d_up, d_rows = [
+        jnp.concatenate([a, b], axis=0) for a, b in zip(own_parts, hot_parts)
+    ]
     all_cotan = jnp.concatenate([own_cotan, hot_cotan], axis=0)
-    normed, hidden = trunk(all_embeds, trunk_gain, trunk_weight)
-    active, d_gate, d_up, d_rows = through_expert(hidden, all_cotan, gate_w, up_w, down_w)
 
     share = feature // n
     block = padded(share, TILE // 2)

time: 122 us -> 124 us (1.016)
  matrix products: 26.9 us -> 22.2 us
  Pallas kernels: 88.3 us -> 92.2 us
  local copies, waits for them, and re-layouts: 1.1 us -> 3.63 us
    pallas_call x1, Pallas kernels: 20.8 us -> 24.8 us  [gather(): pl.pallas_call(functools.partial(gather_kernel, n, experts_axis, width),...]
    dot_general x4, matrix products: 8.3 us -> 5.63 us  [dot_t(): lax.dot_general(a, b, (((1,), (1,)), ((), ())), preferred_element_type=jn...]
    unnamed x11, local copies, waits for them, and re-layouts: 0.94 us -> 2.78 us
where the time goes in v3:
time: 124 us; the launch traced here: 123 us
  Pallas kernels  92.2 us (74%)
  matrix products  22.2 us (18%)
  other arithmetic  3.65 us (3%)
  local copies, waits for them, and re-layouts  3.63 us (3%)
  between operations  1.46 us (1%)
    pallas_call x1, Pallas kernels, exchange(): pl.pallas_call(functools.partial(exchange_kernel, n, experts_axis), out_s...  35.5 us
    pallas_call x1, Pallas kernels, reduce_scatter(): pl.pallas_call(functools.partial(reduce_kernel, n, experts_axis, block, w...  32 us
    pallas_call x1, Pallas kernels, gather(): pl.pallas_call(functools.partial(gather_kernel, n, experts_axis, width),...  24.8 us
    dot_general x3, matrix products, t_dot(): lax.dot_general(a, b, (((0,), (0,)), ((), ())), preferred_element_type=jn...  8.64 us
    dot_general x4, matrix products, dot_t(): lax.dot_general(a, b, (((1,), (1,)), ((), ())), preferred_element_type=jn...  5.63 us
    unnamed x11, local copies, waits for them, and re-layouts  2.78 us

profile of v3, /device:TPU:0, one launch (start us, length us, event | category | flops | bytes accessed | tf_op | source)
XLA Modules:
  0.0 123.2 jit_solution(4944166772414866808)
XLA Ops:
  1.3 1.3 %and_convert_fusion = bf16[256]{0:T(256)(128)(2,1)S(1)} fusion(s32[256]{0:T(256)} %param.18, s32[256]{0:T(256)} %param.16, s32[]{:T(128)} %bitcast.47), kind=kLoop, calls=%fused_computation.100 | loop fusion | flops 1024 | bytes 2564 | tf_op jit(solution)/shard_map/convert_element_type | solution.py:437
  2.6 0.9 convert_reduce_fusion.1
  3.6 0.7 broadcast_add_fusion
  4.3 0.7 broadcast_in_dim.18.refs_2_
  5.1 0.2 iota_compare_fusion.8
  5.2 2.1 %convolution_convert_fusion.3 = bf16[512,1280]{1,0:T(8,128)(2,1)S(1)} fusion(bf16[256,1152]{1,0:T(8,128)(2,1)} %param.19, bf16[256,128]{1,0:T(8,128)(2,1)S(1)} %broadcast_in_dim.16, bf16[256,1152]{1,0:T(8,128)(2,1)} %param.10, pred[512,256]{1,0:T(32,128)(4,1)S(1)} %get-tuple-element.27, pred[512,256]{1,0:T(32,128)(4,1)S(1)} %get-tuple-element.28), kind=kOutput, calls=%fused_computation.8 | convolution fusion | flops 677249024 | bytes 2818048 | tf_op jit(solution)/shard_map/dot_general | solution.py:446
  7.3 35.5 %shard_map.129 = bf16[32,16,1280]{2,1,0:T(8,128)(2,1)S(1)} custom-call(bf16[32,16,1280]{2,1,0:T(8,128)(2,1)S(1)} %bitcast.39), custom_call_target="tpu_custom_call" | custom-call | tf_op jit(solution)/shard_map/pallas_call | solution.py:103
  42.8 0.5 convolution_convert_fusion.7
  43.4 0.1 compare_reduce_fusion
  43.5 0.6 broadcast_select_fusion
  44.1 0.1 convert_reduce_fusion
  44.2 0.2 convolution_convert_fusion.8
  44.4 0.2 convolution_convert_fusion.9
  44.7 24.8 %shard_map.130 = (bf16[32,16,1152]{2,1,0:T(8,128)(2,1)S(1)}, bf16[256,1152]{1,0:T(8,128)(2,1)S(1)}, bf16[256,1152]{1,0:T(8,128)(2,1)S(1)}, bf16[256,1024]{1,0:T(...) custom-call(bf16[16,1152]{1,0:T(8,128)(2,1)S(1)} %pad_maximum_fusion.4., ...), custom_call_target="tpu_custom_call" | custom-call | tf_op jit(solution)/shard_map/pallas_call | solution.py:256
  69.4 0.6 fusion.10
  70.0 0.6 multiply_reduce_fusion
  70.7 0.5 copy-done.3
  71.2 1.1 fusion.9
  72.2 0.2 multiply_convert_fusion
  72.4 3.0 %fusion.4.left_ref = bf16[1280,512]{1,0:T(8,128)(2,1)} fusion(s32[1280]{0:T(1024)S(1)} %fusion.53, bf16[256,1152]{1,0:T(8,128)(2,1)S(1)} %multiply_convert_fusion, bf16[256,1152]{1,0:T(8,128)(2,1)S(1)} %get-tuple-element.16), kind=kOutput, calls=%fused_computation.9 | convolution fusion | flops 1514438656 | bytes 2495488 | tf_op jit(solution)/shard_map/dot_general | solution.py:398
  75.4 0.9 fusion.81
  76.3 0.8 copy-done.2
  77.1 0.9 fusion.74
  78.0 0.8 copy-done.1
  78.7 1.3 %multiply_convert_fusion.1 = (bf16[256,1024]{1,0:T(8,128)(2,1)S(1)}, bf16[256,1024]{1,0:T(8,128)(2,1)S(1)}, bf16[256,1024]{1,0:T(8,128)(2,1)S(1)}) fusion(f32[256,1024]{1,0:T(8,128)S(1)} %fusion.81, f32[256,1024]{1,0:T(8,128)S(1)} %fusion.74, bf16[256,1152]{1,0:T(8,128)(2,1)S(1)} %fusion.9, bf16[1,1152,1024]{2,1,0:T(8,128)(2,1)S(1)} %copy-done.1), kind=kOutput, calls=%fused_computation.51 | convolution fusion | flops 607911936 | bytes 6619136 | tf_op jit(solution)/shard_map/dot_general | solution.py:407
  80.0 3.0 %fusion.3 = bf16[1,1024,1152]{2,1,0:T(8,128)(2,1)} fusion(bf16[256,1152]{1,0:T(8,128)(2,1)S(1)} %fusion.10, bf16[256,1152]{1,0:T(8,128)(2,1)S(1)} %get-tuple-element.23.refs_1_, bf16[256,1024]{1,0:T(8,128)(2,1)S(1)} %get-tuple-element.20, bf16[256,1024]{1,0:T(8,128)(2,1)S(1)} %get-tuple-element.15), kind=kOutput, calls=%fused_computation.7 | convolution fusion | flops 1213595648 | bytes 4587520 | tf_op jit(solution)/shard_map/dot_general | solution.py:402
  83.0 0.9 fusion.79
  83.9 0.9 fusion.8
  84.9 32.0 %shard_map.131 = f32[40,1152]{1,0:T(8,128)S(1)} custom-call(bf16[1280,512]{1,0:T(8,128)(2,1)} %fusion.4.left_ref, bf16[512,1152]{1,0:T(8,128)(2,1)S(1)} %pad_maximum_fusion.1.right_ref), custom_call_target="tpu_custom_call" | custom-call | tf_op jit(solution)/shard_map/pallas_call | solution.py:366
  116.9 2.8 %fusion.2 = bf16[1,1152,1024]{2,1,0:T(8,128)(2,1)} fusion(bf16[256,1024]{1,0:T(8,128)(2,1)S(1)} %get-tuple-element.22, bf16[256,1024]{1,0:T(8,128)(2,1)S(1)} %get-tuple-element.14, bf16[256,1152]{1,0:T(8,128)(2,1)S(1)} %fusion.9, bf16[256,1152]{1,0:T(8,128)(2,1)S(1)} %get-tuple-element.11), kind=kOutput, calls=%fused_computation.6 | convolution fusion | flops 1213595648 | bytes 4587520 | tf_op jit(solution)/shard_map/dot_general | solution.py:402
  119.7 2.8 %fusion.1 = bf16[1,1152,1024]{2,1,0:T(8,128)(2,1)} fusion(bf16[256,1024]{1,0:T(8,128)(2,1)S(1)} %get-tuple-element.21, bf16[256,1024]{1,0:T(8,128)(2,1)S(1)} %get-tuple-element.13, bf16[256,1152]{1,0:T(8,128)(2,1)S(1)} %fusion.9, bf16[256,1152]{1,0:T(8,128)(2,1)S(1)} %get-tuple-element.11), kind=kOutput, calls=%fused_computation.5 | convolution fusion | flops 1213595648 | bytes 4587520 | tf_op jit(solution)/shard_map/dot_general | solution.py:402
  122.6 0.7 copy.19
  (15 shorter events, 0.3 us)
Async XLA Ops:
  69.4 1.8 %copy-start.3 = (bf16[1152,1152]{1,0:T(8,128)(2,1)S(1)}, bf16[1152,1152]{1,0:T(8,128)(2,1)}, u32[]{:S(2)}) copy-start(bf16[1152,1152]{1,0:T(8,128)(2,1)} %refs_3_.1) | copy-start | bytes 7962628
  70.0 1.2 copy-start.4
  72.4 3.0 %copy-start = (bf16[1,1152,1024]{2,1,0:T(8,128)(2,1)S(1)}, bf16[1,1152,1024]{2,1,0:T(8,128)(2,1)}, u32[]{:S(2)}) copy-start(bf16[1,1152,1024]{2,1,0:T(8,128)(2,1)} %param.13) | copy-start | bytes 7077892
  75.4 1.7 %copy-start.2 = (bf16[1,1024,1152]{2,1,0:T(8,128)(2,1)S(1)}, bf16[1,1024,1152]{2,1,0:T(8,128)(2,1)}, u32[]{:S(2)}) copy-start(bf16[1,1024,1152]{2,1,0:T(8,128)(2,1)} %param.15) | copy-start | bytes 7077892
  77.1 1.7 %copy-start.1 = (bf16[1,1152,1024]{2,1,0:T(8,128)(2,1)S(1)}, bf16[1,1152,1024]{2,1,0:T(8,128)(2,1)}, u32[]{:S(2)}) copy-start(bf16[1,1152,1024]{2,1,0:T(8,128)(2,1)} %param.14) | copy-start | bytes 7077892

commit v4 on v2

--- a/solution.py
+++ b/solution.py
@@ -56,11 +56,36 @@
     pl.semaphore_wait(barrier, bits)
 
 
-def exchange_kernel(n, experts_axis, send_ref, out_ref, send_sem, recv_sem, own_sem):
+def exchange_kernel(
+    n, experts_axis, send_ref, mark_ref, out_ref, seen_ref, send_sem, recv_sem, small_send, small_recv, own_sem
+):
     me = flat_index(experts_axis)
     greet_all(n, experts_axis)
     own = pltpu.make_async_copy(send_ref.at[me], out_ref.at[me], own_sem)
     own.start()
+    seen_ref[me] = mark_ref[me]
+
+    def mark_to(step):
+        to = lax.rem(me + step, n)
+        return pltpu.make_async_remote_copy(
+            src_ref=mark_ref.at[to],
+            dst_ref=seen_ref.at[me],
+            send_sem=small_send.at[to],
+            recv_sem=small_recv.at[me],
+            device_id=place(to, experts_axis),
+            device_id_type=MESH,
+        )
+
+    def mark_from(step):
+        source = lax.rem(me + step, n)
+        return pltpu.make_async_remote_copy(
+            src_ref=mark_ref.at[source],
+            dst_ref=seen_ref.at[source],
+            send_sem=small_send.at[source],
+            recv_sem=small_recv.at[source],
+            device_id=place(source, experts_axis),
+            device_id_type=MESH,
+        )
 
     def copy_to(step):
         to = lax.rem(me + step, n)
@@ -86,12 +111,16 @@
 
     def start(step, carry):
         copy_to(step).start()
+        mark_to(step).start()
         return carry
 
     def finish(step, carry):
         copy = copy_from(step)
         copy.wait_send()
         copy.wait_recv()
+        mark = mark_from(step)
+        mark.wait_send()
+        mark.wait_recv()
         return carry
 
     lax.fori_loop(1, n, start, 0)
@@ -99,13 +128,18 @@
     lax.fori_loop(1, n, finish, 0)
 
 
-def exchange(send, n, experts_axis):
+def exchange(send, marks, n, experts_axis):
     return pl.pallas_call(
         functools.partial(exchange_kernel, n, experts_axis),
-        out_shape=jax.ShapeDtypeStruct(send.shape, send.dtype),
-        in_specs=[pl.BlockSpec(memory_space=pltpu.VMEM)],
-        out_specs=pl.BlockSpec(memory_space=pltpu.VMEM),
+        out_shape=[
+            jax.ShapeDtypeStruct(send.shape, send.dtype),
+            jax.ShapeDtypeStruct(marks.shape, marks.dtype),
+        ],
+        in_specs=[pl.BlockSpec(memory_space=pltpu.VMEM)] * 2,
+        out_specs=[pl.BlockSpec(memory_space=pltpu.VMEM)] * 2,
         scratch_shapes=[
+            pltpu.SemaphoreType.DMA((n,)),
+            pltpu.SemaphoreType.DMA((n,)),
             pltpu.SemaphoreType.DMA((n,)),
             pltpu.SemaphoreType.DMA((n,)),
             pltpu.SemaphoreType.DMA,
@@ -113,7 +147,7 @@
         compiler_params=pltpu.CompilerParams(
             collective_id=0, has_side_effects=True, vmem_limit_bytes=40 * 1024 * 1024
         ),
-    )(send)
+    )(send, marks)
 
 
 def axis_orders(n, experts_axis):
@@ -355,21 +389,19 @@
         [line[:, None] == target[None, :], line[:, None] == target[None, :] + capacity], axis=1
     ).astype(jnp.bfloat16)
     flagged = ((tags == hot_expert) & (helper != hot_expert)).astype(jnp.bfloat16)
-    flag_lanes = jnp.broadcast_to(flagged[:, None], (tokens, LANES))
-    content = jnp.concatenate(
-        [
-            jnp.concatenate([embeds, flag_lanes], axis=1),
-            jnp.concatenate([cotangent, jnp.zeros_like(flag_lanes)], axis=1),
-        ],
-        axis=0,
+    lane = jnp.arange(LANES, dtype=jnp.int32)
+    to_device = (helper[None, :] == jnp.arange(n, dtype=jnp.int32)[:, None]).astype(jnp.bfloat16)
+    at_lane = (slot[:, None] == lane[None, :]).astype(jnp.bfloat16) * flagged[:, None]
+    marks = jnp.dot(to_device, at_lane, preferred_element_type=jnp.float32)
+    content = jnp.concatenate([embeds, cotangent], axis=0)
+    send = jnp.dot(pick, content, preferred_element_type=jnp.float32).astype(jnp.bfloat16)
+    got, seen = exchange(
+        send.reshape(n, rows, feature), marks.reshape(n, 1, LANES), n, experts_axis
     )
-    send = jnp.dot(pick, content, preferred_element_type=jnp.float32).astype(jnp.bfloat16)
-    got = exchange(send.reshape(n, rows, feature + LANES), n, experts_axis)
-    got = got.reshape(n * rows, feature + LANES)
-    got_wide = lines_of(got, capacity, rows, 0)
-    got_embeds = got_wide[:, :feature]
-    got_cotan = lines_of(got[:, :feature], capacity, rows, capacity)
-    flags = got_wide[:, feature] > 0
+    got = got.reshape(n * rows, feature)
+    got_embeds = lines_of(got, capacity, rows, 0)
+    got_cotan = lines_of(got, capacity, rows, capacity)
+    flags = seen[:, 0, :capacity].reshape(tokens) > 0
 
     rank = jnp.sum((flags[None, :] & (token[:, None] > token[None, :])).astype(jnp.int32), axis=1)
     picker = (rank[None, :] == jnp.arange(hot_slots, dtype=jnp.int32)[:, None]) & flags[None, :]

time: 122 us -> 125 us (1.025)
  matrix products: 26.9 us -> 30.4 us
  Pallas kernels: 88.3 us -> 86.5 us
    dot_general x4, matrix products: 2.21 us -> 4.74 us  [lines_of(): jnp.dot(chosen.astype(jnp.bfloat16), blocks, preferred_element_type=jnp.f...]
    pallas_call x1, Pallas kernels: 35.5 us -> 33.9 us  [exchange(): pl.pallas_call(functools.partial(exchange_kernel, n, experts_axis), out_s...]
where the time goes in v4:
time: 125 us; the launch traced here: 124 us
  Pallas kernels  86.5 us (69%)
  matrix products  30.4 us (24%)
  other arithmetic  3.65 us (3%)
  local copies, waits for them, and re-layouts  2.05 us (2%)
  between operations  1.61 us (1%)
    pallas_call x1, Pallas kernels, exchange(): pl.pallas_call(functools.partial(exchange_kernel, n, experts_axis), out_s...  33.9 us
    pallas_call x1, Pallas kernels, reduce_scatter(): pl.pallas_call(functools.partial(reduce_kernel, n, experts_axis, block, w...  32 us
    pallas_call x1, Pallas kernels, gather(): pl.pallas_call(functools.partial(gather_kernel, n, experts_axis, width),...  20.6 us
    dot_general x3, matrix products, t_dot(): lax.dot_general(a, b, (((0,), (0,)), ((), ())), preferred_element_type=jn...  8.95 us
    dot_general x4, matrix products, dot_t(): lax.dot_general(a, b, (((1,), (1,)), ((), ())), preferred_element_type=jn...  8.34 us
    dot_general x4, matrix products, lines_of(): jnp.dot(chosen.astype(jnp.bfloat16), blocks, preferred_element_type=jnp.f...  4.74 us

profile of v4, /device:TPU:0, one launch (start us, length us, event | category | flops | bytes accessed | tf_op | source)
XLA Modules:
  0.0 124.2 jit_solution(3542740244795347553)
XLA Ops:
  1.4 1.3 %and_convert_fusion = bf16[256]{0:T(256)(128)(2,1)S(1)} fusion(s32[256]{0:T(256)} %param.18, s32[256]{0:T(256)} %param.16, s32[]{:T(128)} %bitcast.51), kind=kLoop, calls=%fused_computation.102 | loop fusion | flops 1024 | bytes 2564 | tf_op jit(solution)/shard_map/convert_element_type | solution.py:391
  2.8 0.9 convert_reduce_fusion.1
  3.8 0.7 broadcast_add_fusion
  4.5 0.9 fusion.42
  5.4 0.2 iota_compare_fusion.7
  5.5 2.1 %convolution_convert_fusion.3 = bf16[512,1152]{1,0:T(8,128)(2,1)S(1)} fusion(bf16[256,1152]{1,0:T(8,128)(2,1)} %param.19, bf16[256,1152]{1,0:T(8,128)(2,1)} %param.10, pred[512,256]{1,0:T(32,128)(4,1)S(1)} %get-tuple-element.14, pred[512,256]{1,0:T(32,128)(4,1)S(1)} %get-tuple-element.15), kind=kOutput, calls=%fused_computation.14 | convolution fusion | flops 607191040 | bytes 2621440 | tf_op jit(solution)/shard_map/dot_general | solution.py:397
  7.6 33.9 %shard_map.129 = (bf16[32,16,1152]{2,1,0:T(8,128)(2,1)S(1)}, f32[32,1,128]{2,1,0:T(1,128)S(1)}) custom-call(bf16[32,16,1152]{2,1,0:T(8,128)(2,1)S(1)} %bitcast.47, f32[32,1,128]{2,1,0:T(1,128)S(1)} %bitcast.49), custom_call_target="tpu_custom_call" | custom-call | tf_op jit(solution)/shard_map/pallas_call | solution.py:132
  41.5 1.0 copy-done.1
  42.6 0.1 gt.48
  42.7 0.1 convert_reduce_fusion
  42.8 1.8 %convolution_convert_fusion.7 = bf16[256,1152]{1,0:T(8,128)(2,1)S(1)} fusion(bf16[512,1152]{1,0:T(8,128)(2,1)} %bitcast.45, s32[256]{0:T(256)S(1)} %fusion.69), kind=kOutput, calls=%fused_computation.20 | convolution fusion | flops 302415872 | bytes 1770496 | tf_op jit(solution)/shard_map/dot_general | solution.py:338
  44.6 1.8 %broadcast_select_fusion = (bf16[256,1152]{1,0:T(8,128)(2,1)S(1)}, bf16[256,1152]{1,0:T(8,128)(2,1)S(1)}) fusion(pred[256]{0:T(512)(128)(4,1)S(1)} %gt.48, bf16[512,1152]{1,0:T(8,128)(2,1)} %bitcast.46, s32[256]{0:T(256)S(1)} %add_add_fusion), kind=kOutput, calls=%fused_computation.53 | convolution fusion | flops 302710784 | bytes 2360576 | tf_op jit(solution)/shard_map/dot_general | solution.py:338
  46.5 0.2 convolution_convert_fusion.8
  46.7 0.2 convolution_convert_fusion.9
  46.9 20.6 %shard_map.130 = bf16[32,16,1152]{2,1,0:T(8,128)(2,1)S(1)} custom-call(bf16[16,1152]{1,0:T(8,128)(2,1)S(1)} %pad_maximum_fusion.6.mine_ref), custom_call_target="tpu_custom_call" | custom-call | tf_op jit(solution)/shard_map/pallas_call | solution.py:210
  67.5 0.6 fusion.8
  68.1 0.5 convolution_convert_fusion.5
  68.6 0.3 fusion.9
  69.0 1.9 %fusion.4 = bf16[512,1152]{1,0:T(8,128)(2,1)S(1)} fusion(bf16[1152,1152]{1,0:T(8,128)(2,1)S(1)} %copy-done, f32[1152]{0:T(1024)S(1)} %copy-done.5, f32[512]{0:T(512)S(1)} %add_rsqrt_fusion, bf16[256,1152]{1,0:T(8,128)(2,1)S(1)} %convolution_convert_fusion.5, bf16[256,1152]{1,0:T(8,128)(2,1)S(1)} %convolution_convert_fusion.7), kind=kOutput, calls=%fused_computation.12 | convolution fusion | flops 1366622208 | bytes 5020160 | tf_op jit(solution)/shard_map/dot_general | solution.py:347
  70.9 3.1 %fusion.6.left_ref = bf16[1280,512]{1,0:T(8,128)(2,1)} fusion(s32[1280]{0:T(1024)S(1)} %fusion.56, f32[1152]{0:T(1024)S(1)} %copy-done.5, f32[512]{0:T(512)S(1)} %add_rsqrt_fusion, bf16[256,1152]{1,0:T(8,128)(2,1)S(1)} %convolution_convert_fusion.5, bf16[256,1152]{1,0:T(8,128)(2,1)S(1)} %convolution_convert_fusion.7), kind=kOutput, calls=%fused_computation.15 | convolution fusion | flops 1516208128 | bytes 2502144 | tf_op jit(solution)/shard_map/dot_general | solution.py:352
  74.0 1.5 %fusion.14 = f32[512,1024]{1,0:T(8,128)S(1)} fusion(bf16[512,1152]{1,0:T(8,128)(2,1)S(1)} %fusion.4, bf16[1,1152,1024]{2,1,0:T(8,128)(2,1)S(1)} %copy-done.3), kind=kOutput, calls=%fused_computation.27 | convolution fusion | flops 1207959552 | bytes 5636096 | tf_op jit(solution)/shard_map/dot_general | solution.py:360
  75.5 0.1 copy-done.4
  75.7 1.6 %fusion.17 = f32[512,1024]{1,0:T(8,128)S(1)} fusion(bf16[512,1152]{1,0:T(8,128)(2,1)S(1)} %fusion.4, bf16[1,1152,1024]{2,1,0:T(8,128)(2,1)S(1)} %copy-done.4), kind=kOutput, calls=%fused_computation.30 | convolution fusion | flops 1207959552 | bytes 5636096 | tf_op jit(solution)/shard_map/dot_general | solution.py:361
  77.2 0.1 copy-done.2
  77.3 2.1 %multiply_convert_fusion.1 = (bf16[512,1024]{1,0:T(8,128)(2,1)S(1)}, bf16[512,1024]{1,0:T(8,128)(2,1)S(1)}) fusion(f32[512,1024]{1,0:T(8,128)S(1)} %fusion.14, f32[512,1024]{1,0:T(8,128)S(1)} %fusion.17, bf16[1,1024,1152]{2,1,0:T(8,128)(2,1)S(1)} %copy-done.2, bf16[256,1152]{1,0:T(8,128)(2,1)S(1)} %fusion.8, bf16[256,1152]{1,0:T(8,128)(2,1)S(1)} %get-tuple-element.12), kind=kOutput, calls=%fused_computation.37 | convolution fusion | flops 1217134592 | bytes 9830400 | tf_op jit(solution)/shard_map/dot_general | solution.py:352
  79.4 3.1 %fusion.3 = bf16[1,1024,1152]{2,1,0:T(8,128)(2,1)} fusion(f32[512,1024]{1,0:T(8,128)S(1)} %fusion.17, bf16[256,1152]{1,0:T(8,128)(2,1)S(1)} %fusion.8, bf16[256,1152]{1,0:T(8,128)(2,1)S(1)} %get-tuple-element.12, f32[512,1024]{1,0:T(8,128)S(1)} %fusion.14), kind=kOutput, calls=%fused_computation.11 | convolution fusion | flops 1214644224 | bytes 7733248 | tf_op jit(solution)/shard_map/dot_general | solution.py:356
  82.5 3.0 %fusion.2 = bf16[1,1152,1024]{2,1,0:T(8,128)(2,1)} fusion(bf16[512,1152]{1,0:T(8,128)(2,1)S(1)} %fusion.4, bf16[512,1024]{1,0:T(8,128)(2,1)S(1)} %get-tuple-element.10), kind=kOutput, calls=%fused_computation.10 | convolution fusion | flops 1209139200 | bytes 4587520 | tf_op jit(solution)/shard_map/dot_general | solution.py:356
  85.5 2.8 %fusion.1 = bf16[1,1152,1024]{2,1,0:T(8,128)(2,1)} fusion(bf16[512,1152]{1,0:T(8,128)(2,1)S(1)} %fusion.4, bf16[512,1024]{1,0:T(8,128)(2,1)S(1)} %get-tuple-element.11), kind=kOutput, calls=%fused_computation.9 | convolution fusion | flops 1209139200 | bytes 4587520 | tf_op jit(solution)/shard_map/dot_general | solution.py:356
  88.4 1.6 %fusion.12 = f32[512,1152]{1,0:T(8,128)S(1)} fusion(bf16[512,1024]{1,0:T(8,128)(2,1)S(1)} %get-tuple-element.11, bf16[1,1152,1024]{2,1,0:T(8,128)(2,1)S(1)} %copy-done.3), kind=kOutput, calls=%fused_computation.25 | convolution fusion | flops 1207959552 | bytes 5767168 | tf_op jit(solution)/shard_map/dot_general | solution.py:352
  89.9 1.6 %fusion.5.right_ref = bf16[512,1152]{1,0:T(8,128)(2,1)S(1)} fusion(f32[512,1152]{1,0:T(8,128)S(1)} %fusion.12, bf16[512,1024]{1,0:T(8,128)(2,1)S(1)} %get-tuple-element.10, bf16[1,1152,1024]{2,1,0:T(8,128)(2,1)S(1)} %copy-done.4), kind=kOutput, calls=%fused_computation.13 | convolution fusion | flops 1209139200 | bytes 6946816 | tf_op jit(solution)/shard_map/dot_general | solution.py:352
  91.5 32.0 %shard_map.131 = f32[40,1152]{1,0:T(8,128)S(1)} custom-call(bf16[1280,512]{1,0:T(8,128)(2,1)} %fusion.6.left_ref, bf16[512,1152]{1,0:T(8,128)(2,1)S(1)} %fusion.5.right_ref), custom_call_target="tpu_custom_call" | custom-call | tf_op jit(solution)/shard_map/pallas_call | solution.py:320
  123.6 0.7 copy.19
  (15 shorter events, 0.1 us)
Async XLA Ops:
  0.6 68.3 %copy-start = (bf16[1152,1152]{1,0:T(8,128)(2,1)S(1)}, bf16[1152,1152]{1,0:T(8,128)(2,1)}, u32[]{:S(2)}) copy-start(bf16[1152,1152]{1,0:T(8,128)(2,1)} %param.12) | copy-start | bytes 7962628
  41.5 1.0 copy-start.1
  67.5 1.5 %copy-start.5 = (f32[1152]{0:T(1024)S(1)}, f32[1152]{0:T(1024)}, u32[]{:S(2)}) copy-start(f32[1152]{0:T(1024)} %param.11) | copy-start | bytes 13828
  70.9 3.1 %copy-start.3 = (bf16[1,1152,1024]{2,1,0:T(8,128)(2,1)S(1)}, bf16[1,1152,1024]{2,1,0:T(8,128)(2,1)}, u32[]{:S(2)}) copy-start(bf16[1,1152,1024]{2,1,0:T(8,128)(2,1)} %param.13) | copy-start | bytes 7077892
  74.0 1.7 %copy-start.4 = (bf16[1,1152,1024]{2,1,0:T(8,128)(2,1)S(1)}, bf16[1,1152,1024]{2,1,0:T(8,128)(2,1)}, u32[]{:S(2)}) copy-start(bf16[1,1152,1024]{2,1,0:T(8,128)(2,1)} %param.14) | copy-start | bytes 7077892
  75.7 1.7 %copy-start.2 = (bf16[1,1024,1152]{2,1,0:T(8,128)(2,1)S(1)}, bf16[1,1024,1152]{2,1,0:T(8,128)(2,1)}, u32[]{:S(2)}) copy-start(bf16[1,1024,1152]{2,1,0:T(8,128)(2,1)} %param.15) | copy-start | bytes 7077892
